TPU v7x, 128 devices: a whole 4x4x4 slice. The times are simulated.
128 devices in a mesh: cell: 64 (over x, y, z_lo, core), rank: 2 (over z_hi).
Axes of the slice: x: 4, y: 4, z: 4 (z_hi: 2, z_lo: 2; z = z_hi * 2 + z_lo), core: 2. Of those that a mesh axis runs over, the one named last changes fastest.
Arguments:
- factors: float32 [48, 256, 2048], P(None, 'cell', 'rank'), may hold values from -1.7 to 1.7
- rank_weights: float32 [2048], P('rank'), may hold values from 0.5 to 2
- triples: int32 [2, 3], replicated, may hold values from 0 to 47, as said below
- targets: bfloat16 [2, 256, 256, 256], P(None, 'cell'), may hold values from -6 to 6
Outputs:
- new_factors: float32 [48, 256, 2048], P(None, 'cell', 'rank')
Inputs may be any that keep to these rules, and one draw needn't show every extreme that they name: `triples`: the three attributes of a table are different.
All inputs are finite; a program needn't handle non-finite values.
Results may differ from a plain program's by a relative error of at most 0.0022.
Values may be sent and summed in bfloat16 or wider, within the bound.
A program may use at most 64 MiB of HBM per device.

v0:
```python
import jax
import jax.numpy as jnp
from jax import lax
from jax.sharding import PartitionSpec as P

learn_rate = 0.02


def place(gradient, attr_ids, attribute, term):
    return gradient + jnp.where((attr_ids == attribute)[:, None, None], term[None], 0.0)


def on_device(factors, rank_weights, triples, targets):
    tables = triples.shape[0]
    attrs, levels_dev, rank_dev = factors.shape
    levels = targets.shape[2]
    attr_ids = lax.iota(jnp.int32, attrs)
    gradient = jnp.zeros(factors.shape, jnp.float32)
    for table in range(tables):
        first_attr = triples[table, 0]
        second_attr = triples[table, 1]
        third_attr = triples[table, 2]
        own_first = factors[first_attr]
        gathered = lax.all_gather(
            jnp.stack([factors[second_attr], factors[third_attr]]), "cell", axis=1, tiled=True
        )
        full_second = gathered[0]
        full_third = gathered[1]
        second_bf = full_second.astype(jnp.bfloat16)
        third_bf = full_third.astype(jnp.bfloat16)
        scaled = ((rank_weights * own_first)[:, None, :] * full_second[None]).astype(jnp.bfloat16)
        partial_model = lax.dot_general(
            scaled.reshape(levels_dev * levels, rank_dev),
            third_bf,
            (((1,), (1,)), ((), ())),
            preferred_element_type=jnp.float32,
        )
        model = lax.psum(partial_model, "rank")
        resid = (
            model.reshape(levels_dev, levels, levels) - targets[table].astype(jnp.float32)
        ).astype(jnp.bfloat16)
        xprod = jnp.einsum("ijk,kr->ijr", resid, third_bf, preferred_element_type=jnp.float32)
        grad_first = rank_weights * jnp.sum(xprod * full_second[None], axis=1)
        gradient = place(gradient, attr_ids, first_attr, grad_first)
        vprod = jnp.einsum("ijk,jr->ikr", resid, second_bf, preferred_element_type=jnp.float32)
        term_second = rank_weights * jnp.sum(xprod * own_first[:, None, :], axis=0)
        term_third = rank_weights * jnp.sum(vprod * own_first[:, None, :], axis=0)
        summed = lax.psum_scatter(
            jnp.stack([term_second, term_third], axis=1), "cell", scatter_dimension=0, tiled=True
        )
        grad_second = summed[:, 0]
        grad_third = summed[:, 1]
        gradient = place(gradient, attr_ids, second_attr, grad_second)
        gradient = place(gradient, attr_ids, third_attr, grad_third)
    return factors - learn_rate * gradient


def solution(mesh):
    in_specs = (P(None, "cell", "rank"), P("rank"), P(), P(None, "cell", None, None))
    out_specs = P(None, "cell", "rank")
    return jax.shard_map(
        on_device, mesh=mesh, in_specs=in_specs, out_specs=out_specs, check_vma=False
    )
```

profile of v0, /device:TPU:1, one launch (start us, length us, event | category | flops | bytes accessed | tf_op | source)
XLA Modules:
  0.0 889.0 jit_solution(5531718622913671323)
XLA Ops:
  6.5 1.6 fusion.15
  22.2 101.6 %all-gather.3.cloned.1.call-done = f32[2,256,1024]{2,0,1:T(2,128)} async-done(((f32[2,4,1024]{2,0,1:T(2,128)}), f32[2,256,1024]{2,0,1:T(2,128)}) %all-gather.3.cloned.1.call-update) | async-done | bytes 2097168 | tf_op jit(solution)/shard_map/all_gather | solution.py:24
  123.8 2.3 slice.66
  126.4 101.5 %all-gather.5.cloned.1.call-done = f32[2,256,1024]{2,0,1:T(2,128)} async-done(((f32[2,4,1024]{2,0,1:T(2,128)}), f32[2,256,1024]{2,0,1:T(2,128)}) %all-gather.5.cloned.1.call-update) | async-done | bytes 2097168 | tf_op jit(solution)/shard_map/all_gather | solution.py:24
  227.9 2.3 slice.68
  230.4 1.2 multiply_convert_fusion
  232.4 1.1 slice.69
  233.5 1.0 copy-done.7
  234.5 1.8 fusion.8
  236.2 1.1 slice.67
  237.3 1.0 copy-done.5
  238.3 1.7 fusion.12
  240.3 2.2 fusion.14
  242.5 67.7 %all-reduce.9.cloned.1.call-done = (f32[1024,256]{1,0:T(8,128)}, f32[1024,256]{1,0:T(8,128)}) async-done(((f32[1024,256]{1,0:T(8,128)}, f32[1024,256]{1,0:T(8,128)}), (f32[1024,256]{1,0:T(8,128)}, f32[1024,256]{1,0:T(8,128)})) %all-reduce.9.cloned.1.call-update) | async-done | bytes 2097168 | tf_op jit(solution)/shard_map/psum | solution.py:38
  310.2 1.6 fusion
  312.2 1.0 multiply_reduce_fusion.2
  314.9 0.9 multiply_reduce_fusion.5
  317.5 1.5 pad_maximum_fusion
  319.0 1.5 pad_maximum_fusion.1
  322.4 1.2 iota_compare_fusion.4
  323.6 1.3 iota_compare_fusion.2
  324.9 1.2 iota_compare_fusion
  326.1 553.0 %all-reduce.7.cloned.1.call-done = (f32[256,2,1024]{2,0,1:T(8,128)}, f32[256,2,1024]{2,0,1:T(8,128)}) async-done(((f32[256,2,1024]{2,0,1:T(8,128)}, f32[256,2,1024]{2,0,1:T(8,128)}), (f32[256,2,1024]{2,0,1:T(8,128)}, f32[256,2,1024]{2,0,1:T(8,128)})) %all-reduce.7.cloned.1.call-update) | async-done | bytes 4194320
  880.7 1.8 multiply_subtract_fusion
  (50 shorter events, 10.9 us)
Async XLA Ops:
  6.5 117.3 %all-gather.3.cloned.1.call-start = ((), (), s32[]{:S(2)}) async-start(), calls=%async_computation | async-start | bytes 2129920 | tf_op jit(solution)/shard_map/all_gather | solution.py:24
  16.9 211.0 %all-gather.5.cloned.1.call-start = ((), (), s32[]{:S(2)}) async-start(), calls=%async_computation.1 | async-start | bytes 2129920 | tf_op jit(solution)/shard_map/all_gather | solution.py:24
  17.6 292.6 %all-reduce.9.cloned.1.call-start = ((), (), s32[]{:S(2)}) async-start(), calls=%async_computation.3 | async-start | bytes 4194304 | tf_op jit(solution)/shard_map/psum | solution.py:38
  230.4 1.3 copy-start
  230.4 2.0 copy-start.3
  233.5 1.0 copy-start.7
  234.5 1.8 copy-start.2
  237.3 1.0 copy-start.5
  240.1 639.1 %all-reduce.7.cloned.1.call-start = ((), (), s32[]{:S(2)}) async-start(), calls=%async_computation.2 | async-start | bytes 8388608
  310.2 1.7 copy-start.1
  310.2 2.0 copy-start.8
  313.2 1.0 copy-start.4
  313.2 1.4 copy-start.9
  313.2 1.7 copy-start.6
  315.9 0.8 copy-start.11
  320.5 0.7 copy-start.12
  320.5 560.2 %copy-start.10 = (f32[48,4,1024]{2,1,0:T(4,128)S(1)}, f32[48,4,1024]{2,1,0:T(4,128)}, u32[]{:S(2)}) copy-start(f32[48,4,1024]{2,1,0:T(4,128)} %param.4) | copy-start | bytes 2359300
Sparse Core Ops, SparseCore 0:
  17.0 106.7 all-gather.2
  125.6 102.3 all-gather.4
  240.2 69.9 all-reduce.8
  320.7 558.4 all-reduce.6
where the time goes:
time: 890 us; the launch traced here: 889 us
  waiting for transfers between devices  824 us (93%)
  between operations  25.1 us (3%)
  local copies, waits for them, and re-layouts  18.4 us (2%)
  other arithmetic  14.4 us (2%)
    unnamed x5, waiting for transfers between devices  553 us
    all_gather x2, waiting for transfers between devices, on_device(): lax.all_gather(jnp.stack([factors[second_attr], factors[third_attr]]), 'c...  203 us
    psum x1, waiting for transfers between devices, on_device(): model = lax.psum(partial_model, 'rank')  67.7 us
  transfers between devices with their start and end apart: 4, of which 4 were waited for; matrix products, arithmetic and copies ran while one was open for 1% of the time, Pallas kernels for 0%

commit v1 on v0

v1 whole, which is shorter than its diff:
```python
import functools

import jax
import jax.numpy as jnp
from jax import lax
from jax.experimental import pallas as pl
from jax.experimental.pallas import tpu as pltpu
from jax.sharding import PartitionSpec as P

learn_rate = 0.02
MESH = pl.DeviceIdType.MESH
f32, bf16 = jnp.float32, jnp.bfloat16


def cell_of(x, y, zl, core):
    return ((x * 4 + y) * 2 + zl) * 2 + core


def rcopy(src, dst, send_sem, recv_sem, cell, rank):
    return pltpu.make_async_remote_copy(
        src_ref=src, dst_ref=dst, send_sem=send_sem, recv_sem=recv_sem,
        device_id={"cell": cell, "rank": rank}, device_id_type=MESH)


def kernel(tri, w, fac, tgt, out, msg, col, bfull, cfull, wa, tg, scaled, pm_own, pm_send, pm_recv, ga, gb, gc,
           gb_send, gc_send, b1, c1, b1_send, c1_send, b2, c2, fsend, frecv, full,
           t_local, t_sem, col_s, col_r, g1_s, g1_r, g2_s, g2_r, pm_s, pm_r, r1_s, r1_r, r2_s, r2_r, f_s, f_r):
    cell = lax.axis_index("cell")
    zh = lax.axis_index("rank")
    core = cell % 2
    zl = (cell // 2) % 2
    y = (cell // 4) % 4
    x = cell // 16
    rows = w.shape[1]

    barrier = pltpu.get_barrier_semaphore()
    for dz in range(2):
        for dl in range(2):
            for dc in range(2):
                if dz or dl or dc:
                    pl.semaphore_signal(
                        barrier, inc=1, device_id_type=MESH,
                        device_id={"cell": cell_of(x, y, (zl + dl) % 2, (core + dc) % 2), "rank": (zh + dz) % 2})
    for d in range(1, 4):
        pl.semaphore_signal(barrier, inc=1, device_id_type=MESH,
                            device_id={"cell": cell_of((x + d) % 4, y, zl, core), "rank": zh})
        pl.semaphore_signal(barrier, inc=1, device_id_type=MESH,
                            device_id={"cell": cell_of(x, (y + d) % 4, zl, core), "rank": zh})

    own_tgt = pltpu.make_async_copy(tgt.at[zh], tg.at[pl.ds(core * 4, 4)], t_local)
    own_tgt.start()
    for t in range(2):
        a = w[...] * fac[tri[t, 0]]
        b = fac[tri[t, 1]]
        c = fac[tri[t, 2]]
        hi = a.astype(bf16).astype(f32)
        msg[t] = jnp.concatenate([hi, b, c, a - hi], axis=0).astype(bf16)
    pl.semaphore_wait(barrier, 13)

    slot = zl * 2 + core
    for t in range(2):
        for dl in range(2):
            to_l = (zl + dl) % 2
            is_self = (dl == 0) & (core == zh) & (zh == t)

            @pl.when(jnp.logical_not(is_self))
            def _():
                rcopy(msg.at[t], col.at[slot], col_s.at[t * 2 + dl], col_r.at[slot], cell_of(x, y, to_l, zh), t).start()

            if dl == 0:
                @pl.when(is_self)
                def _():
                    col[slot] = msg[t]
    tg_copy = rcopy(tgt.at[zh], tg.at[pl.ds(core * 4, 4)], t_sem.at[0], t_sem.at[1], cell_of(x, y, zl, 1 - core), zh)
    tg_copy.start()
    for s in range(4):
        from_self = (core == zh) & (slot == s)

        @pl.when(jnp.logical_not(from_self))
        def _():
            rcopy(msg.at[0], col.at[s], col_s.at[0], col_r.at[s], cell_of(x, y, zl, 1 - core), zh).wait_recv()
    got = [col[s].astype(f32) for s in range(4)]
    bfull[x, y] = jnp.concatenate([m[4:8] for m in got], axis=0).astype(bf16)
    cfull[x, y] = jnp.concatenate([m[8:12] for m in got], axis=0).astype(bf16)
    own = [col[zl * 2 + c].astype(f32) for c in range(2)]
    wa[...] = jnp.concatenate([m[0:4] + m[12:16] for m in own], axis=0)

    first = []
    for d in range(1, 4):
        first.append(rcopy(bfull.at[x, y], bfull.at[x, y], g1_s.at[d], g1_r.at[d], cell_of((x + d) % 4, y, zl, core), zh))
        first.append(rcopy(cfull.at[x, y], cfull.at[x, y], g1_s.at[4 + d], g1_r.at[4 + d], cell_of(x, (y + d) % 4, zl, core), zh))
    for copy in first:
        copy.start()
    for d in range(1, 4):
        bx, cy = (x + 4 - d) % 4, (y + 4 - d) % 4
        rcopy(bfull.at[bx, y], bfull.at[bx, y], g1_s.at[d], g1_r.at[d], cell_of(bx, y, zl, core), zh).wait_recv()
        rcopy(cfull.at[x, cy], cfull.at[x, cy], g1_s.at[4 + d], g1_r.at[4 + d], cell_of(x, cy, zl, core), zh).wait_recv()
    for copy in first:
        copy.wait_send()

    up_y, dn_y = cell_of(x, (y + 1) % 4, zl, core), cell_of(x, (y + 3) % 4, zl, core)
    up_x, dn_x = cell_of((x + 1) % 4, y, zl, core), cell_of((x + 3) % 4, y, zl, core)

    def half(ref, which, part, h):
        return ref.at[pl.ds(2 * h, 2), part] if which == 0 else ref.at[part, pl.ds(2 * h, 2)]

    def second(which, k, part, h, to):
        ref = (bfull, cfull)[which]
        view = half(ref, which, part, h)
        return rcopy(view, view, g2_s.at[which * 6 + k], g2_r.at[which * 6 + k], to, zh)

    pos = (y, x)
    ups, dns = (up_y, up_x), (dn_y, dn_x)
    sent = []
    for k in range(2):
        for which in range(2):
            sent.append(second(which, k, pos[which], k, ups[which]))
            sent.append(second(which, 2 + k, pos[which], 1 - k, dns[which]))
    for copy in sent:
        copy.start()
    forwards = []
    for which in range(2):
        below, above = (pos[which] + 3) % 4, (pos[which] + 1) % 4
        second(which, 0, below, 0, dns[which]).wait_recv()
        forwards.append(second(which, 4, below, 0, ups[which]))
        forwards[-1].start()
        second(which, 2, above, 1, ups[which]).wait_recv()
        forwards.append(second(which, 5, above, 1, dns[which]))
        forwards[-1].start()
    for which in range(2):
        below, above, far = (pos[which] + 3) % 4, (pos[which] + 1) % 4, (pos[which] + 2) % 4
        second(which, 1, below, 1, dns[which]).wait_recv()
        second(which, 3, above, 0, ups[which]).wait_recv()
        second(which, 4, far, 0, dns[which]).wait_recv()
        second(which, 5, far, 1, ups[which]).wait_recv()
    for copy in sent + forwards:
        copy.wait_send()

    other = cell_of(x, y, zl, 1 - core)

    def pm_copy(i):
        return rcopy(pm_send.at[i], pm_recv.at[i], pm_s.at[i], pm_r.at[i], other, zh)

    @pl.loop(0, 8)
    def _(i):
        s = (wa[pl.ds(i, 1), :] * bfull[...].reshape(256, rows).astype(f32)).astype(bf16)
        scaled[i] = s
        pm = lax.dot_general(s, cfull[...].reshape(256, rows), (((1,), (1,)), ((), ())), preferred_element_type=f32)
        pm_own[i] = pm
        pm_send[i] = pm.astype(bf16)
        pm_copy(i).start()

    own_tgt.wait()
    tg_copy.wait_send()
    rcopy(tgt.at[zh], tg.at[pl.ds((1 - core) * 4, 4)], t_sem.at[0], t_sem.at[1], other, zh).wait_recv()

    gb[...] = jnp.zeros_like(gb)
    gc[...] = jnp.zeros_like(gc)

    @pl.loop(0, 8)
    def _(i):
        pm_copy(i).wait_recv()
        r = (pm_own[i] + pm_recv[i].astype(f32) - tg[i].astype(f32)).astype(bf16)
        xprod = jnp.dot(r, cfull[...].reshape(256, rows), preferred_element_type=f32)
        ga[pl.ds(i, 1), :] = jnp.sum(xprod * bfull[...].reshape(256, rows).astype(f32), axis=0, keepdims=True)
        gb[...] += wa[pl.ds(i, 1), :] * xprod
        gc[...] += lax.dot_general(r, scaled[i], (((0,), (0,)), ((), ())), preferred_element_type=f32)

    @pl.loop(0, 8)
    def _(i):
        pm_copy(i).wait_send()

    gb_send[...] = gb[...].reshape(4, 4, 16, rows).astype(bf16)
    gc_send[...] = gc[...].reshape(4, 4, 16, rows).astype(bf16)
    first = []
    for d in range(1, 4):
        ty, tx = (y + d) % 4, (x + d) % 4
        first.append(rcopy(gb_send.at[:, ty], b1.at[d - 1], r1_s.at[d], r1_r.at[d], cell_of(x, ty, zl, core), zh))
        first.append(rcopy(gc_send.at[tx], c1.at[d - 1], r1_s.at[4 + d], r1_r.at[4 + d], cell_of(tx, y, zl, core), zh))
    for copy in first:
        copy.start()
    for copy in first:
        copy.wait_recv()
    for q in range(4):
        @pl.when(y == q)
        def _():
            full[0] = gb[...].reshape(4, 4, 16, rows)[:, q]

        @pl.when(x == q)
        def _():
            full[1] = gc[...].reshape(4, 4, 16, rows)[q]
    full[0] += b1[0].astype(f32) + b1[1].astype(f32) + b1[2].astype(f32)
    full[1] += c1[0].astype(f32) + c1[1].astype(f32) + c1[2].astype(f32)
    b1_send[...] = full[0].astype(bf16)
    c1_send[...] = full[1].astype(bf16)
    for copy in first:
        copy.wait_send()
    last = []
    for d in range(1, 4):
        ty, tx = (y + d) % 4, (x + d) % 4
        last.append(rcopy(b1_send.at[tx], b2.at[d - 1], r2_s.at[d], r2_r.at[d], cell_of(tx, y, zl, core), zh))
        last.append(rcopy(c1_send.at[ty], c2.at[d - 1], r2_s.at[4 + d], r2_r.at[4 + d], cell_of(x, ty, zl, core), zh))
    for copy in last:
        copy.start()
    for copy in last:
        copy.wait_recv()
    sum_b = full[0, x] + b2[0].astype(f32) + b2[1].astype(f32) + b2[2].astype(f32)
    sum_c = full[1, y] + c2[0].astype(f32) + c2[1].astype(f32) + c2[2].astype(f32)
    for copy in last:
        copy.wait_send()

    grad_a = ga[...]
    for s in range(4):
        c = s % 2
        ga4 = grad_a[4 * c:4 * c + 4]
        ga4 = jnp.where(zl == s // 2, ga4, 0.0)
        fsend[s] = jnp.concatenate([sum_b[4 * s:4 * s + 4], sum_c[4 * s:4 * s + 4], ga4, jnp.zeros_like(ga4)], axis=0)
    fslot = zl * 2 + zh
    for s in range(4):
        is_self = (slot == s) & (zh == core)

        @pl.when(jnp.logical_not(is_self))
        def _():
            rcopy(fsend.at[s], frecv.at[fslot], f_s.at[s], f_r.at[fslot], cell_of(x, y, s // 2, s % 2), core).start()

        @pl.when(is_self)
        def _():
            frecv[fslot] = fsend[s]
    for s in range(4):
        from_self = (fslot == s) & (zh == core)

        @pl.when(jnp.logical_not(from_self))
        def _():
            rcopy(fsend.at[0], frecv.at[s], f_s.at[0], f_r.at[s], other, zh).wait_recv()
    grads = []
    for t in range(2):
        g = learn_rate * (frecv[t] + frecv[2 + t])
        grads.append((tri[t, 0], w[...] * g[8:12]))
        grads.append((tri[t, 1], g[0:4]))
        grads.append((tri[t, 2], g[4:8]))

    @pl.loop(0, 48)
    def _(attr):
        step = jnp.zeros((4, rows), f32)
        for which, g in grads:
            step = step + jnp.where(which == attr, g, 0.0)
        out[attr] = fac[attr] - step

    for t in range(2):
        for dl in range(2):
            is_self = (dl == 0) & (core == zh) & (zh == t)

            @pl.when(jnp.logical_not(is_self))
            def _():
                rcopy(msg.at[t], col.at[slot], col_s.at[t * 2 + dl], col_r.at[slot], other, t).wait_send()
    for s in range(4):
        is_self = (slot == s) & (zh == core)

        @pl.when(jnp.logical_not(is_self))
        def _():
            rcopy(fsend.at[s], frecv.at[fslot], f_s.at[s], f_r.at[fslot], other, core).wait_send()


def on_device(factors, rank_weights, triples, targets):
    rows = rank_weights.shape[0]
    vmem = pl.BlockSpec(memory_space=pltpu.VMEM)
    dma = pltpu.SemaphoreType.DMA
    V = pltpu.VMEM
    return pl.pallas_call(
        kernel,
        out_shape=jax.ShapeDtypeStruct(factors.shape, f32),
        in_specs=[pl.BlockSpec(memory_space=pltpu.SMEM), vmem, vmem, pl.BlockSpec(memory_space=pl.ANY)],
        out_specs=vmem,
        scratch_shapes=[
            V((2, 16, rows), bf16),
            V((4, 16, rows), bf16),
            V((4, 4, 16, rows), bf16),
            V((4, 4, 16, rows), bf16),
            V((8, rows), f32),
            V((8, 256, 256), bf16),
            V((8, 256, rows), bf16),
            V((8, 256, 256), f32),
            V((8, 256, 256), bf16),
            V((8, 256, 256), bf16),
            V((8, rows), f32),
            V((256, rows), f32),
            V((256, rows), f32),
            V((4, 4, 16, rows), bf16),
            V((4, 4, 16, rows), bf16),
            V((3, 4, 16, rows), bf16),
            V((3, 4, 16, rows), bf16),
            V((4, 16, rows), bf16),
            V((4, 16, rows), bf16),
            V((3, 16, rows), bf16),
            V((3, 16, rows), bf16),
            V((4, 16, rows), f32),
            V((4, 16, rows), f32),
            V((2, 4, 16, rows), f32),
            dma, dma((2,)), dma((4,)), dma((4,)), dma((8,)), dma((8,)), dma((12,)), dma((12,)),
            dma((8,)), dma((8,)), dma((8,)), dma((8,)), dma((8,)), dma((8,)), dma((4,)), dma((4,)),
        ],
        compiler_params=pltpu.CompilerParams(collective_id=0, has_side_effects=True, vmem_limit_bytes=56 * 1024 * 1024),
    )(triples, rank_weights.reshape(1, rows), factors, targets)


def solution(mesh):
    in_specs = (P(None, "cell", "rank"), P("rank"), P(), P(None, "cell", None, None))
    return jax.shard_map(on_device, mesh=mesh, in_specs=in_specs, out_specs=P(None, "cell", "rank"), check_vma=False)
```

time: 890 us -> 54.7 us (0.06)
  waiting for transfers between devices: 824 us -> 0 us
  Pallas kernels: 0 us -> 52.4 us
  between operations: 25.1 us -> 0.01 us
  local copies, waits for them, and re-layouts: 18.4 us -> 2.06 us
  other arithmetic: 14.4 us -> 0 us
    unnamed x5 -> x0, waiting for transfers between devices: 553 us -> none
    all_gather x2 -> x0, waiting for transfers between devices: 203 us -> none  [on_device(): lax.all_gather(jnp.stack([factors[second_attr], factors[third_attr]]), 'c...]
    psum x1 -> x0, waiting for transfers between devices: 67.7 us -> none  [on_device(): model = lax.psum(partial_model, 'rank')]
    pallas_call x0 -> x1, Pallas kernels: none -> 52.4 us  [on_device(): pl.pallas_call(kernel, out_shape=jax.ShapeDtypeStruct(factors.shape, f32)...]
    slice x6 -> x0, local copies, waits for them, and re-layouts: 10.6 us -> none  [the longest x2 4.62 us: on_device(): full_second = gathered[0]]
  transfers between devices with their start and end apart: 4 -> 0, of which waited for: 4 -> 0; matrix products, arithmetic and copies ran while one was open for 1% -> 0% of each run, Pallas kernels for 0% -> 0%
where the time goes in v1:
time: 54.7 us; the launch traced here: 54.5 us
  Pallas kernels  52.4 us (96%)
  local copies, waits for them, and re-layouts  2.06 us (4%)
    pallas_call x1, Pallas kernels, on_device(): pl.pallas_call(kernel, out_shape=jax.ShapeDtypeStruct(factors.shape, f32)...  52.4 us
    unnamed x1, local copies, waits for them, and re-layouts  2.06 us

profile of v1, /device:TPU:1, one launch (start us, length us, event | category | flops | bytes accessed | tf_op | source)
XLA Modules:
  0.0 54.5 jit_solution(8469730501075975561)
XLA Ops:
  0.0 52.4 %shard_map.46 = f32[48,4,1024]{2,1,0:T(4,128)} custom-call(s32[2,3]{1,0:T(2,128)} %tri.1, f32[1,1024]{1,0:T(1,128)} %bitcast.1, f32[48,4,1024]{2,1,0:T(4,128)} %fac.1, bf16[2,4,256,256]{3,2,1,0:T(8,128)(2,1)} %tgt.1), custom_call_target="tpu_custom_call" | custom-call | tf_op jit(solution)/shard_map/pallas_call | solution.py:269
  52.4 2.1 %copy.6 = f32[48,4,1024]{2,1,0:T(4,128)} copy(f32[48,4,1024]{2,1,0:T(4,128)} %shard_map.46) | data formatting | bytes 1572864

commit v2 on v0

v2 whole, which is shorter than its diff:
```python
import jax
import jax.numpy as jnp
from jax import lax
from jax.experimental import pallas as pl
from jax.experimental.pallas import tpu as pltpu
from jax.sharding import PartitionSpec as P

learn_rate = 0.02
MESH = pl.DeviceIdType.MESH
f32, bf16 = jnp.float32, jnp.bfloat16
NT = (((1,), (1,)), ((), ()))


def cell_of(x, y, zl, core):
    return ((x * 4 + y) * 2 + zl) * 2 + core


def rcopy(src, dst, send_sem, recv_sem, cell, rank):
    return pltpu.make_async_remote_copy(
        src_ref=src, dst_ref=dst, send_sem=send_sem, recv_sem=recv_sem,
        device_id={"cell": cell, "rank": rank}, device_id_type=MESH)


def unless(flag):
    return pl.when(jnp.logical_not(flag))


def kernel(tri, w, fac_hbm, tgt, out, fac, msg, amsg, col, acol, bfull, cfull, wa, tg, scaled, pm_own, pm_send, pm_recv,
           resid, resid_t, ga, gb, gc, gb_send, gc_send, b1, c1, b2_send, c2_send, b2, c2, asend, arecv,
           l_sem, t_sem, col_s, col_r, acol_s, acol_r, g_s, g_r, pm_s, pm_r, r_s, r_r, f_s, f_r, a_s, a_r):
    cell = lax.axis_index("cell")
    zh = lax.axis_index("rank")
    core = cell % 2
    zl = (cell // 2) % 2
    y = (cell // 4) % 4
    x = cell // 16
    rows = w.shape[1]
    hw = rows // 2
    me = cell_of(x, y, zl, core)
    other = cell_of(x, y, zl, 1 - core)

    load = pltpu.make_async_copy(fac_hbm, fac, l_sem.at[0])
    load.start()
    own_tgt = pltpu.make_async_copy(tgt.at[zh], tg.at[pl.ds(core * 4, 4)], l_sem.at[1])
    own_tgt.start()

    barrier = pltpu.get_barrier_semaphore()

    def greet(to, rank):
        pl.semaphore_signal(barrier, inc=1, device_id={"cell": to, "rank": rank}, device_id_type=MESH)

    for s in range(4):
        @unless((zl == s // 2) & (core == s % 2) & (zh == core))
        def _():
            greet(cell_of(x, y, s // 2, s % 2), core)

    @pl.when(zh != core)
    def _():
        greet(other, zh)
    for d in range(1, 4):
        greet(cell_of((x + d) % 4, y, zl, core), zh)
        greet(cell_of(x, (y + d) % 4, zl, core), zh)

    load.wait()
    for t in range(2):
        a = w[...] * fac[tri[t, 0]]
        b = fac[tri[t, 1]]
        c = fac[tri[t, 2]]
        hi = a.astype(bf16).astype(f32)
        lo = a - hi
        msg[t] = jnp.concatenate([b[:, :hw], c[:, :hw], b[:, hw:], c[:, hw:]], axis=0).astype(bf16)
        amsg[t] = jnp.concatenate([hi[:, :hw], lo[:, :hw], hi[:, hw:], lo[:, hw:]], axis=0).astype(bf16)
    pl.semaphore_wait(barrier, 10)

    slot = zl * 2 + core

    def col_copy(t, dl):
        return rcopy(msg.at[t], col.at[slot], col_s.at[t * 2 + dl], col_r.at[slot], cell_of(x, y, (zl + dl) % 2, zh), t)

    def acol_copy(t):
        return rcopy(amsg.at[t], acol.at[core], acol_s.at[t], acol_r.at[core], cell_of(x, y, zl, zh), t)

    for dl in (1, 0):
        for t in range(2):
            if dl == 1:
                col_copy(t, dl).start()
            else:
                is_self = (core == zh) & (zh == t)

                @unless(is_self)
                def _():
                    col_copy(t, dl).start()
                    acol_copy(t).start()

                @pl.when(is_self)
                def _():
                    col[slot] = msg[t]
                    acol[core] = amsg[t]
    for s in range(4):
        @unless((core == zh) & (slot == s))
        def _():
            rcopy(msg.at[0], col.at[s], col_s.at[0], col_r.at[s], other, zh).wait_recv()
    got = [col[s].astype(f32) for s in range(4)]
    for h in range(2):
        bfull[h, x, y] = jnp.concatenate([m[8 * h:8 * h + 4] for m in got], axis=0).astype(bf16)
        cfull[h, x, y] = jnp.concatenate([m[8 * h + 4:8 * h + 8] for m in got], axis=0).astype(bf16)

    first_pos, second_pos = (x, y), (y, x)

    def block(which, h, p, q):
        return bfull.at[h, p, q] if which == 0 else cfull.at[h, q, p]

    def along_first(which, d):
        return cell_of((x + d) % 4, y, zl, core) if which == 0 else cell_of(x, (y + d) % 4, zl, core)

    def along_second(which, d):
        return along_first(1 - which, d)

    def gather_copy(which, h, p, q, k, to):
        view = block(which, h, p % 4, q % 4)
        n = (which * 2 + h) * 16 + k
        return rcopy(view, view, g_s.at[n], g_r.at[n], to, zh)

    gathers = []

    def send(*args):
        gathers.append(gather_copy(*args))
        gathers[-1].start()

    def first(which, h, d):
        send(which, h, first_pos[which], second_pos[which], d, along_first(which, d))

    def first_wait(which, h, d):
        gather_copy(which, h, first_pos[which] + 4 - d, second_pos[which], d, other).wait_recv()

    def near(which, h, e):
        for up in (1, 0):
            send(which, h, first_pos[which] + e, second_pos[which], 4 + 2 * e + up, along_second(which, 1 if up else 3))

    def near_wait(which, h, e, up):
        gather_copy(which, h, first_pos[which] + e, second_pos[which] + (3 if up else 1), 4 + 2 * e + up, other).wait_recv()

    def forward(which, h, e):
        up = 1 if e in (0, 2) else 0
        near_wait(which, h, e, up)
        send(which, h, first_pos[which] + e, second_pos[which] + (3 if up else 1), 12 + e, along_second(which, 1 if up else 3))

    def far_wait(which, h, e):
        gather_copy(which, h, first_pos[which] + e, second_pos[which] + 2, 12 + e, other).wait_recv()

    both = [(which, h) for h in range(2) for which in range(2)]
    for d in (2, 1, 3):
        for which, h in both:
            first(which, h, d)
    for which, h in both:
        near(which, h, 0)

    tg_copy = rcopy(tgt.at[zh], tg.at[pl.ds(core * 4, 4)], t_sem.at[0], t_sem.at[1], other, zh)
    tg_copy.start()
    for c in range(2):
        @unless((core == zh) & (core == c))
        def _():
            rcopy(amsg.at[0], acol.at[c], acol_s.at[0], acol_r.at[c], other, zh).wait_recv()
    got = [acol[c].astype(f32) for c in range(2)]
    for h in range(2):
        wa[:, h * hw:(h + 1) * hw] = jnp.concatenate([m[8 * h:8 * h + 4] + m[8 * h + 4:8 * h + 8] for m in got], axis=0)

    for d in (1, 3):
        for which, h in both:
            first_wait(which, h, d)
            near(which, h, 4 - d)
    for which, h in both:
        first_wait(which, h, 2)
        near(which, h, 2)
    for e in (0, 1, 3, 2):
        for which, h in both:
            forward(which, h, e)

    def pm_copy(i):
        return rcopy(pm_send.at[i], pm_recv.at[i], pm_s.at[i], pm_r.at[i], other, zh)

    for h in range(2):
        for which in range(2):
            for e, up in ((0, 0), (1, 1), (3, 1), (2, 0)):
                near_wait(which, h, e, up)
        for e in (0, 1, 3, 2):
            for which in range(2):
                far_wait(which, h, e)

        @pl.loop(0, 8)
        def _(i):
            wrow = wa[pl.ds(i, 1), h * hw:(h + 1) * hw]
            s = (wrow * bfull[h].reshape(256, hw).astype(f32)).astype(bf16)
            scaled[h, pl.ds(pl.multiple_of(i * 256, 256), 256), :] = s
            pm = lax.dot_general(s, cfull[h].reshape(256, hw), NT, preferred_element_type=f32)
            if h == 0:
                pm_own[i] = pm
            else:
                pm = pm_own[i] + pm
                pm_own[i] = pm
                pm_send[i] = pm.astype(bf16)
                pm_copy(i).start()

    own_tgt.wait()
    rcopy(tgt.at[zh], tg.at[pl.ds((1 - core) * 4, 4)], t_sem.at[0], t_sem.at[1], other, zh).wait_recv()

    @pl.loop(0, 8)
    def _(i):
        pm_copy(i).wait_recv()
        r = (pm_own[i] + pm_recv[i].astype(f32) - tg[i].astype(f32)).astype(bf16)
        at = pl.multiple_of(i * 256, 256)
        resid[pl.ds(at, 256), :] = r
        resid_t[:, pl.ds(at, 256)] = r.T

    scatters = []

    def scatter(src, dst, which, h, d, to):
        n = (which * 2 + h) * 4 + d
        scatters.append(rcopy(src, dst, r_s.at[n], r_r.at[n], to, zh))
        scatters[-1].start()

    def scatter_wait(which, h, d):
        n = (which * 2 + h) * 4 + d
        dst = (b1, c1)[which].at[h, d - 1]
        rcopy(dst, dst, r_s.at[n], r_r.at[n], other, zh).wait_recv()

    for h in range(2):
        part = jnp.dot(resid_t[...], scaled[h], preferred_element_type=f32)
        gc[h] = part.reshape(4, 4, 16, hw)
        gc_send[h] = part.reshape(4, 4, 16, hw).astype(bf16)
        for d in (2, 1, 3):
            scatter(gc_send.at[h, (x + d) % 4], c1.at[h, d - 1], 1, h, d, cell_of((x + d) % 4, y, zl, core))

        @pl.loop(0, 2)
        def _(q):
            lanes = pl.ds(pl.multiple_of(q * 256, 256), 256)
            wlanes = pl.ds(pl.multiple_of(h * hw + q * 256, 256), 256)
            cs = cfull[h, :, :, :, lanes].reshape(256, 256)
            bs = bfull[h, :, :, :, lanes].reshape(256, 256).astype(f32)
            acc = jnp.zeros((256, 256), f32)
            for i in range(8):
                xprod = jnp.dot(resid[i * 256:(i + 1) * 256, :], cs, preferred_element_type=f32)
                ga[i:i + 1, wlanes] = jnp.sum(xprod * bs, axis=0, keepdims=True)
                acc = acc + wa[i:i + 1, wlanes] * xprod
            gb[h, :, :, :, lanes] = acc.reshape(4, 4, 16, 256)
            gb_send[h, :, :, :, lanes] = acc.reshape(4, 4, 16, 256).astype(bf16)
        for d in (2, 1, 3):
            scatter(gb_send.at[h, :, (y + d) % 4], b1.at[h, d - 1], 0, h, d, cell_of(x, (y + d) % 4, zl, core))

    def a_copy(c):
        return rcopy(asend.at[c], arecv.at[zh], a_s.at[c], a_r.at[zh], cell_of(x, y, zl, c), core)

    for c in range(2):
        asend[c] = jnp.concatenate([ga[4 * c:4 * c + 4, :hw], ga[4 * c:4 * c + 4, hw:]], axis=0)
        is_self = (core == c) & (zh == core)

        @unless(is_self)
        def _():
            a_copy(c).start()

        @pl.when(is_self)
        def _():
            arecv[zh] = asend[c]

    def final_copy(which, h, d, s, to_wait=False):
        buf_s, buf_r = ((b2_send, b2), (c2_send, c2))[which]
        p = first_pos[which]
        n = (which * 2 + h) * 16
        if which == 0:
            to = cell_of((x + d) % 4, y, s // 2, s % 2)
        else:
            to = cell_of(x, (y + d) % 4, s // 2, s % 2)
        at = (p * 2 + zl) * 2 + zh
        return rcopy(buf_s.at[h, (p + d) % 4, s], buf_r.at[h, at], f_s.at[n + d * 4 + s], f_r.at[n + at], to, core)

    def final_self(d, s):
        return (zl == s // 2) & (core == s % 2) & (zh == core) if d == 0 else None

    order = [(1, 0), (0, 0), (1, 1), (0, 1)]
    for which, h in order:
        for d in (1, 3, 2):
            scatter_wait(which, h, d)
        if which == 0:
            total = gb[h, :, y] + b1[h, 0].astype(f32) + b1[h, 1].astype(f32) + b1[h, 2].astype(f32)
        else:
            total = gc[h, x] + c1[h, 0].astype(f32) + c1[h, 1].astype(f32) + c1[h, 2].astype(f32)
        buf_s, buf_r = ((b2_send, b2), (c2_send, c2))[which]
        for p in range(4):
            for s in range(4):
                buf_s[h, p, s] = jnp.concatenate(
                    [total[p, 4 * s:4 * s + 4, 128 * q:128 * q + 128] for q in range(4)], axis=0).astype(bf16)
        for d in (2, 1, 3, 0):
            for s in range(4):
                if d:
                    final_copy(which, h, d, s).start()
                else:
                    @unless(final_self(d, s))
                    def _():
                        final_copy(which, h, d, s).start()

                    @pl.when(final_self(d, s))
                    def _():
                        buf_r[h, (first_pos[which] * 2 + zl) * 2 + zh] = buf_s[h, first_pos[which], s]

    for c in range(2):
        @unless((c == zh) & (zh == core))
        def _():
            rcopy(asend.at[0], arecv.at[c], a_s.at[0], a_r.at[c], other, zh).wait_recv()
    sums = {}
    for which, h in order:
        buf_r = (b2, c2)[which]
        for d in (0, 1, 3, 2):
            for k in range(4):
                at = ((first_pos[which] + d) % 4) * 4 + k
                n = (which * 2 + h) * 16 + at
                take = rcopy(buf_r.at[h, at], buf_r.at[h, at], f_s.at[0], f_r.at[n], other, zh)
                if d:
                    take.wait_recv()
                else:
                    @unless((zl == k // 2) & (zh == k % 2) & (zh == core))
                    def _():
                        take.wait_recv()
        for t in range(2):
            total = sum(buf_r[h, 2 * k + t].astype(f32) for k in range(8))
            sums[which, h, t] = jnp.concatenate([total[4 * q:4 * q + 4] for q in range(4)], axis=1)
    steps = []
    for t in range(2):
        g = arecv[t]
        steps.append((tri[t, 0], learn_rate * (w[...] * jnp.concatenate([g[0:4], g[4:8]], axis=1))))
        for which in range(2):
            g = jnp.concatenate([sums[which, 0, t], sums[which, 1, t]], axis=1)
            steps.append((tri[t, 1 + which], learn_rate * g))

    @pl.loop(0, 48)
    def _(attr):
        step = jnp.zeros((4, rows), f32)
        for which, g in steps:
            step = step + jnp.where(which == attr, g, 0.0)
        out[attr] = fac[attr] - step

    for t in range(2):
        col_copy(t, 1).wait_send()

        @unless((core == zh) & (zh == t))
        def _():
            col_copy(t, 0).wait_send()
            acol_copy(t).wait_send()
    tg_copy.wait_send()
    for copy in gathers + scatters:
        copy.wait_send()

    @pl.loop(0, 8)
    def _(i):
        pm_copy(i).wait_send()
    for c in range(2):
        @unless((core == c) & (zh == core))
        def _():
            a_copy(c).wait_send()
    for which, h in order:
        for d in range(4):
            for s in range(4):
                if d:
                    final_copy(which, h, d, s).wait_send()
                else:
                    @unless(final_self(d, s))
                    def _():
                        final_copy(which, h, d, s).wait_send()


def on_device(factors, rank_weights, triples, targets):
    rows = rank_weights.shape[0]
    hw = rows // 2
    vmem = pl.BlockSpec(memory_space=pltpu.VMEM)
    hbm = pl.BlockSpec(memory_space=pl.ANY)
    dma = pltpu.SemaphoreType.DMA
    V = pltpu.VMEM
    return pl.pallas_call(
        kernel,
        out_shape=jax.ShapeDtypeStruct(factors.shape, f32),
        in_specs=[pl.BlockSpec(memory_space=pltpu.SMEM), vmem, hbm, hbm],
        out_specs=vmem,
        scratch_shapes=[
            V(factors.shape, f32),
            V((2, 16, hw), bf16),
            V((2, 16, hw), bf16),
            V((4, 16, hw), bf16),
            V((2, 16, hw), bf16),
            V((2, 4, 4, 16, hw), bf16),
            V((2, 4, 4, 16, hw), bf16),
            V((8, rows), f32),
            V((8, 256, 256), bf16),
            V((2, 2048, hw), bf16),
            V((8, 256, 256), f32),
            V((8, 256, 256), bf16),
            V((8, 256, 256), bf16),
            V((2048, 256), bf16),
            V((256, 2048), bf16),
            V((8, rows), f32),
            V((2, 4, 4, 16, hw), f32),
            V((2, 4, 4, 16, hw), f32),
            V((2, 4, 4, 16, hw), bf16),
            V((2, 4, 4, 16, hw), bf16),
            V((2, 3, 4, 16, hw), bf16),
            V((2, 3, 4, 16, hw), bf16),
            V((2, 4, 4, 16, 128), bf16),
            V((2, 4, 4, 16, 128), bf16),
            V((2, 16, 16, 128), bf16),
            V((2, 16, 16, 128), bf16),
            V((2, 8, hw), f32),
            V((2, 8, hw), f32),
            dma((2,)), dma((2,)), dma((4,)), dma((4,)), dma((2,)), dma((2,)), dma((64,)), dma((64,)),
            dma((8,)), dma((8,)), dma((16,)), dma((16,)), dma((64,)), dma((64,)), dma((2,)), dma((2,)),
        ],
        compiler_params=pltpu.CompilerParams(collective_id=0, has_side_effects=True, vmem_limit_bytes=56 * 1024 * 1024),
    )(triples, rank_weights.reshape(1, rows), factors, targets)


def solution(mesh):
    in_specs = (P(None, "cell", "rank"), P("rank"), P(), P(None, "cell", None, None))
    return jax.shard_map(on_device, mesh=mesh, in_specs=in_specs, out_specs=P(None, "cell", "rank"), check_vma=False)
```

time: 890 us -> 50.8 us (0.06)
  waiting for transfers between devices: 824 us -> 0 us
  Pallas kernels: 0 us -> 48.6 us
  between operations: 25.1 us -> 0.01 us
  local copies, waits for them, and re-layouts: 18.4 us -> 2.06 us
  other arithmetic: 14.4 us -> 0 us
    unnamed x5 -> x0, waiting for transfers between devices: 553 us -> none
    all_gather x2 -> x0, waiting for transfers between devices: 203 us -> none  [on_device(): lax.all_gather(jnp.stack([factors[second_attr], factors[third_attr]]), 'c...]
    psum x1 -> x0, waiting for transfers between devices: 67.7 us -> none  [on_device(): model = lax.psum(partial_model, 'rank')]
    pallas_call x0 -> x1, Pallas kernels: none -> 48.6 us  [on_device(): pl.pallas_call(kernel, out_shape=jax.ShapeDtypeStruct(factors.shape, f32)...]
    slice x6 -> x0, local copies, waits for them, and re-layouts: 10.6 us -> none  [the longest x2 4.62 us: on_device(): full_second = gathered[0]]
  transfers between devices with their start and end apart: 4 -> 0, of which waited for: 4 -> 0; matrix products, arithmetic and copies ran while one was open for 1% -> 0% of each run, Pallas kernels for 0% -> 0%
where the time goes in v2:
time: 50.8 us; the launch traced here: 50.6 us
  Pallas kernels  48.6 us (96%)
  local copies, waits for them, and re-layouts  2.06 us (4%)
    pallas_call x1, Pallas kernels, on_device(): pl.pallas_call(kernel, out_shape=jax.ShapeDtypeStruct(factors.shape, f32)...  48.6 us
    unnamed x1, local copies, waits for them, and re-layouts  2.06 us

profile of v2, /device:TPU:1, one launch (start us, length us, event | category | flops | bytes accessed | tf_op | source)
XLA Modules:
  0.0 50.6 jit_solution(2521817042825605644)
XLA Ops:
  0.0 48.6 %shard_map.46 = f32[48,4,1024]{2,1,0:T(4,128)} custom-call(s32[2,3]{1,0:T(2,128)} %tri.1, f32[1,1024]{1,0:T(1,128)} %bitcast.1, f32[48,4,1024]{2,1,0:T(4,128)} %fac_hbm.1, bf16[2,4,256,256]{3,2,1,0:T(8,128)(2,1)} %tgt.1), custom_call_target="tpu_custom_call" | custom-call | tf_op jit(solution)/shard_map/pallas_call | solution.py:377
  48.6 2.1 %copy.6 = f32[48,4,1024]{2,1,0:T(4,128)} copy(f32[48,4,1024]{2,1,0:T(4,128)} %shard_map.46) | data formatting | bytes 1572864

commit v3 on v2

v3 whole, which is shorter than its diff:
```python
import jax
import jax.numpy as jnp
from jax import lax
from jax.experimental import pallas as pl
from jax.experimental.pallas import tpu as pltpu
from jax.sharding import PartitionSpec as P

learn_rate = 0.02
MESH = pl.DeviceIdType.MESH
f32, bf16 = jnp.float32, jnp.bfloat16
NT = (((1,), (1,)), ((), ()))


def cell_of(x, y, zl, core):
    return ((x * 4 + y) * 2 + zl) * 2 + core


def rcopy(src, dst, send_sem, recv_sem, cell, rank):
    return pltpu.make_async_remote_copy(
        src_ref=src, dst_ref=dst, send_sem=send_sem, recv_sem=recv_sem,
        device_id={"cell": cell, "rank": rank}, device_id_type=MESH)


def arrived(ref, sem):
    rcopy(ref, ref, sem, sem, 0, 0).wait_recv()


def unless(flag):
    return pl.when(jnp.logical_not(flag))


def kernel(tri, w, fac_hbm, tgt, out, fac, msg, amsg, col, acol, bfull, cfull, wa, tg, scaled, pm_own, pm_send, pm_recv,
           resid, resid_t, ga, gb, gc, gb_send, gc_send, b1, c1, b2_send, c2_send, b2, c2, asend, arecv,
           l_sem, t_sem, sent, col_r, first_r, near_r, far_r, pm_r, r_r, f_r):
    cell = lax.axis_index("cell")
    zh = lax.axis_index("rank")
    core = cell % 2
    zl = (cell // 2) % 2
    y = (cell // 4) % 4
    x = cell // 16
    rows = w.shape[1]
    hw = rows // 2
    me = cell_of(x, y, zl, core)
    other = cell_of(x, y, zl, 1 - core)

    load = pltpu.make_async_copy(fac_hbm, fac, l_sem.at[0])
    load.start()
    own_tgt = pltpu.make_async_copy(tgt.at[zh], tg.at[pl.ds(core * 4, 4)], l_sem.at[1])
    own_tgt.start()

    barrier = pltpu.get_barrier_semaphore()

    def greet(to, rank):
        pl.semaphore_signal(barrier, inc=1, device_id={"cell": to, "rank": rank}, device_id_type=MESH)

    for s in range(4):
        @unless((zl == s // 2) & (core == s % 2) & (zh == core))
        def _():
            greet(cell_of(x, y, s // 2, s % 2), core)

    @pl.when(zh != core)
    def _():
        greet(other, zh)
    for d in range(1, 4):
        greet(cell_of((x + d) % 4, y, zl, core), zh)
        greet(cell_of(x, (y + d) % 4, zl, core), zh)

    load.wait()
    for t in range(2):
        a = w[...] * fac[tri[t, 0]]
        b = fac[tri[t, 1]]
        c = fac[tri[t, 2]]
        hi = a.astype(bf16).astype(f32)
        lo = a - hi
        msg[t] = jnp.concatenate([b[:, :hw], c[:, :hw], b[:, hw:], c[:, hw:]], axis=0).astype(bf16)
        amsg[t] = jnp.concatenate([hi[:, :hw], lo[:, :hw], hi[:, hw:], lo[:, hw:]], axis=0).astype(bf16)
    pl.semaphore_wait(barrier, 10)

    slot = zl * 2 + core

    def col_copy(t, dl):
        return rcopy(msg.at[t], col.at[slot], sent.at[0], col_r.at[0], cell_of(x, y, (zl + dl) % 2, zh), t)

    def acol_copy(t):
        return rcopy(amsg.at[t], acol.at[core], sent.at[0], col_r.at[1], cell_of(x, y, zl, zh), t)

    for dl in (1, 0):
        for t in range(2):
            if dl == 1:
                col_copy(t, dl).start()
            else:
                is_self = (core == zh) & (zh == t)

                @unless(is_self)
                def _():
                    col_copy(t, dl).start()
                    acol_copy(t).start()

                @pl.when(is_self)
                def _():
                    col[slot] = msg[t]
                    acol[core] = amsg[t]

    @unless(core == zh)
    def _():
        arrived(col, col_r.at[0])

    @pl.when(core == zh)
    def _():
        arrived(col.at[pl.ds(0, 3)], col_r.at[0])

    got = [col[s].astype(f32) for s in range(4)]
    for h in range(2):
        bfull[h, x, y] = jnp.concatenate([m[8 * h:8 * h + 4] for m in got], axis=0).astype(bf16)
        cfull[h, x, y] = jnp.concatenate([m[8 * h + 4:8 * h + 8] for m in got], axis=0).astype(bf16)

    first_pos, second_pos = (x, y), (y, x)

    def block(which, h, p, q):
        return bfull.at[h, p, q] if which == 0 else cfull.at[h, q, p]

    def along_first(which, d):
        return cell_of((x + d) % 4, y, zl, core) if which == 0 else cell_of(x, (y + d) % 4, zl, core)

    def along_second(which, d):
        return along_first(1 - which, d)

    def send(which, h, p, q, recv_sem, to):
        view = block(which, h, p % 4, q % 4)
        rcopy(view, view, sent.at[1], recv_sem, to, zh).start()

    def first(which, d):
        view = block(which, slice(None), first_pos[which], second_pos[which])
        rcopy(view, view, sent.at[1], first_r.at[which * 3 + d - 1], along_first(which, d), zh).start()

    def first_wait(which, d):
        arrived(block(which, slice(None), (first_pos[which] + 4 - d) % 4, second_pos[which]), first_r.at[which * 3 + d - 1])

    passed_on = {1: (0, 2), 0: (1, 3)}

    def near_sem(which, h, e, up):
        return near_r.at[(which * 2 + h) * 5 + (e if e in passed_on[up] else 4)]

    def near(which, h, e):
        for up in (1, 0):
            send(which, h, first_pos[which] + e, second_pos[which], near_sem(which, h, e, up), along_second(which, 1 if up else 3))

    def forward(which, h, e):
        up = 1 if e in passed_on[1] else 0
        p, q = first_pos[which] + e, second_pos[which] + (3 if up else 1)
        arrived(block(which, h, p % 4, q % 4), near_sem(which, h, e, up))
        send(which, h, p, q, far_r.at[which * 2 + h], along_second(which, 1 if up else 3))

    both = [(which, h) for h in range(2) for which in range(2)]
    for d in (2, 1, 3):
        for which in range(2):
            first(which, d)
    for which, h in both:
        near(which, h, 0)

    tg_copy = rcopy(tgt.at[zh], tg.at[pl.ds(core * 4, 4)], t_sem.at[0], t_sem.at[1], other, zh)
    tg_copy.start()

    @unless(core == zh)
    def _():
        arrived(acol, col_r.at[1])

    @pl.when(core == zh)
    def _():
        arrived(acol.at[0], col_r.at[1])

    got = [acol[c].astype(f32) for c in range(2)]
    for h in range(2):
        wa[:, h * hw:(h + 1) * hw] = jnp.concatenate([m[8 * h:8 * h + 4] + m[8 * h + 4:8 * h + 8] for m in got], axis=0)

    for d in (1, 3, 2):
        for which in range(2):
            first_wait(which, d)
            near(which, 0, 4 - d)
            near(which, 1, 4 - d)
    for e in (0, 1, 3, 2):
        for which, h in both:
            forward(which, h, e)

    def pm_copy(i):
        part = pl.ds(i, 2)
        return rcopy(pm_send.at[part], pm_recv.at[part], sent.at[2], pm_r.at[i // 2], other, zh)

    for h in range(2):
        for which in range(2):
            arrived(bfull.at[h, 0], near_r.at[(which * 2 + h) * 5 + 4])
            arrived(bfull.at[h, 0], far_r.at[which * 2 + h])
        bs = bfull[h].reshape(256, hw).astype(f32)
        cs = cfull[h].reshape(256, hw)
        for i in range(8):
            s = (wa[i:i + 1, h * hw:(h + 1) * hw] * bs).astype(bf16)
            scaled[h, i * 256:(i + 1) * 256, :] = s
            pm = lax.dot_general(s, cs, NT, preferred_element_type=f32)
            if h == 0:
                pm_own[i] = pm
            else:
                pm = pm_own[i] + pm
                pm_own[i] = pm
                pm_send[i] = pm.astype(bf16)
                if i % 2:
                    pm_copy(i - 1).start()

    own_tgt.wait()
    arrived(tg.at[pl.ds((1 - core) * 4, 4)], t_sem.at[1])

    for i in range(8):
        if i % 2 == 0:
            arrived(pm_recv.at[pl.ds(i, 2)], pm_r.at[i // 2])
        r = (pm_own[i] + pm_recv[i].astype(f32) - tg[i].astype(f32)).astype(bf16)
        resid[i * 256:(i + 1) * 256, :] = r
        resid_t[:, i * 256:(i + 1) * 256] = r.T

    def scatter(src, dst, which, h, to):
        rcopy(src, dst, sent.at[3], r_r.at[which * 2 + h], to, zh).start()

    for h in range(2):
        for q in range(2):
            lanes = slice(q * 256, (q + 1) * 256)
            wlanes = slice(h * hw + q * 256, h * hw + (q + 1) * 256)
            part = jnp.dot(resid_t[...], scaled[h, :, lanes], preferred_element_type=f32).reshape(4, 4, 16, 256)
            gc[h, q] = part
            gc_send[h, q] = part.astype(bf16)
            for d in (2, 1, 3):
                scatter(gc_send.at[h, q, (x + d) % 4], c1.at[h, d - 1, q], 1, h, cell_of((x + d) % 4, y, zl, core))
            cs = cfull[h, :, :, :, lanes].reshape(256, 256)
            bs = bfull[h, :, :, :, lanes].reshape(256, 256).astype(f32)
            acc = jnp.zeros((256, 256), f32)
            for i in range(8):
                xprod = jnp.dot(resid[i * 256:(i + 1) * 256, :], cs, preferred_element_type=f32)
                ga[i:i + 1, wlanes] = jnp.sum(xprod * bs, axis=0, keepdims=True)
                acc = acc + wa[i:i + 1, wlanes] * xprod
            acc = acc.reshape(4, 4, 16, 256)
            gb[h, q] = acc
            gb_send[h, q] = acc.astype(bf16)
            for d in (2, 1, 3):
                scatter(gb_send.at[h, q, :, (y + d) % 4], b1.at[h, d - 1, q], 0, h, cell_of(x, (y + d) % 4, zl, core))

    def a_copy(c):
        return rcopy(asend.at[c], arecv.at[zh], sent.at[4], col_r.at[2], cell_of(x, y, zl, c), core)

    for c in range(2):
        asend[c] = jnp.concatenate([ga[4 * c:4 * c + 4, :hw], ga[4 * c:4 * c + 4, hw:]], axis=0)
        is_self = (core == c) & (zh == core)

        @unless(is_self)
        def _():
            a_copy(c).start()

        @pl.when(is_self)
        def _():
            arecv[zh] = asend[c]

    def final_copy(which, h, d, s):
        buf_s, buf_r = ((b2_send, b2), (c2_send, c2))[which]
        p = first_pos[which]
        if which == 0:
            to = cell_of((x + d) % 4, y, s // 2, s % 2)
        else:
            to = cell_of(x, (y + d) % 4, s // 2, s % 2)
        at = (p * 2 + zl) * 2 + zh
        return rcopy(buf_s.at[h, (p + d) % 4, s], buf_r.at[h, at], sent.at[5], f_r.at[which * 2 + h], to, core)

    def final_self(d, s):
        return (zl == s // 2) & (core == s % 2) & (zh == core) if d == 0 else None

    order = [(1, 0), (0, 0), (1, 1), (0, 1)]
    for which, h in order:
        buf, mine = (b1, gb[h, :, :, y]) if which == 0 else (c1, gc[h, :, x])
        arrived(buf.at[h], r_r.at[which * 2 + h])
        total = mine + buf[h, 0].astype(f32) + buf[h, 1].astype(f32) + buf[h, 2].astype(f32)
        buf_s, buf_r = ((b2_send, b2), (c2_send, c2))[which]
        for p in range(4):
            for s in range(4):
                buf_s[h, p, s] = jnp.concatenate(
                    [total[q // 2, p, 4 * s:4 * s + 4, 128 * (q % 2):128 * (q % 2) + 128] for q in range(4)], axis=0).astype(bf16)
        for d in (2, 1, 3, 0):
            for s in range(4):
                if d:
                    final_copy(which, h, d, s).start()
                else:
                    @unless(final_self(d, s))
                    def _():
                        final_copy(which, h, d, s).start()

                    @pl.when(final_self(d, s))
                    def _():
                        buf_r[h, (first_pos[which] * 2 + zl) * 2 + zh] = buf_s[h, first_pos[which], s]

    @unless(zh == core)
    def _():
        arrived(arecv, col_r.at[2])

    @pl.when(zh == core)
    def _():
        arrived(arecv.at[0], col_r.at[2])

    sums = {}
    for which, h in order:
        buf_r = (b2, c2)[which]

        @unless(zh == core)
        def _():
            arrived(buf_r.at[h], f_r.at[which * 2 + h])

        @pl.when(zh == core)
        def _():
            arrived(buf_r.at[h, pl.ds(0, 15)], f_r.at[which * 2 + h])

        for t in range(2):
            total = sum(buf_r[h, 2 * k + t].astype(f32) for k in range(8))
            sums[which, h, t] = jnp.concatenate([total[4 * q:4 * q + 4] for q in range(4)], axis=1)
    steps = []
    for t in range(2):
        g = arecv[t]
        steps.append((tri[t, 0], learn_rate * (w[...] * jnp.concatenate([g[0:4], g[4:8]], axis=1))))
        for which in range(2):
            g = jnp.concatenate([sums[which, 0, t], sums[which, 1, t]], axis=1)
            steps.append((tri[t, 1 + which], learn_rate * g))

    @pl.loop(0, 48)
    def _(attr):
        step = jnp.zeros((4, rows), f32)
        for which, g in steps:
            step = step + jnp.where(which == attr, g, 0.0)
        out[attr] = fac[attr] - step

    def left(ref, k):
        rcopy(ref, ref, sent.at[k], sent.at[k], 0, 0).wait_send()

    tg_copy.wait_send()
    left(scaled.at[0, pl.ds(0, 960)], 1)
    left(pm_send, 2)
    left(scaled.at[0, pl.ds(0, 768)], 3)

    @unless(zh == core)
    def _():
        left(scaled.at[0, pl.ds(0, 96)], 0)
        left(asend, 4)
        left(scaled.at[0, pl.ds(0, 256)], 5)

    @pl.when(zh == core)
    def _():
        left(scaled.at[0, pl.ds(0, 64)], 0)
        left(asend.at[0], 4)
        left(scaled.at[0, pl.ds(0, 240)], 5)


def on_device(factors, rank_weights, triples, targets):
    rows = rank_weights.shape[0]
    hw = rows // 2
    vmem = pl.BlockSpec(memory_space=pltpu.VMEM)
    hbm = pl.BlockSpec(memory_space=pl.ANY)
    dma = pltpu.SemaphoreType.DMA
    V = pltpu.VMEM
    return pl.pallas_call(
        kernel,
        out_shape=jax.ShapeDtypeStruct(factors.shape, f32),
        in_specs=[pl.BlockSpec(memory_space=pltpu.SMEM), vmem, hbm, hbm],
        out_specs=vmem,
        scratch_shapes=[
            V(factors.shape, f32),
            V((2, 16, hw), bf16),
            V((2, 16, hw), bf16),
            V((4, 16, hw), bf16),
            V((2, 16, hw), bf16),
            V((2, 4, 4, 16, hw), bf16),
            V((2, 4, 4, 16, hw), bf16),
            V((8, rows), f32),
            V((8, 256, 256), bf16),
            V((2, 2048, hw), bf16),
            V((8, 256, 256), f32),
            V((8, 256, 256), bf16),
            V((8, 256, 256), bf16),
            V((2048, 256), bf16),
            V((256, 2048), bf16),
            V((8, rows), f32),
            V((2, 2, 4, 4, 16, 256), f32),
            V((2, 2, 4, 4, 16, 256), f32),
            V((2, 2, 4, 4, 16, 256), bf16),
            V((2, 2, 4, 4, 16, 256), bf16),
            V((2, 3, 2, 4, 16, 256), bf16),
            V((2, 3, 2, 4, 16, 256), bf16),
            V((2, 4, 4, 16, 128), bf16),
            V((2, 4, 4, 16, 128), bf16),
            V((2, 16, 16, 128), bf16),
            V((2, 16, 16, 128), bf16),
            V((2, 8, hw), f32),
            V((2, 8, hw), f32),
            dma((2,)), dma((2,)), dma((6,)), dma((3,)), dma((6,)), dma((20,)), dma((4,)), dma((4,)), dma((4,)), dma((4,)),
        ],
        compiler_params=pltpu.CompilerParams(collective_id=0, has_side_effects=True, vmem_limit_bytes=56 * 1024 * 1024),
    )(triples, rank_weights.reshape(1, rows), factors, targets)


def solution(mesh):
    in_specs = (P(None, "cell", "rank"), P("rank"), P(), P(None, "cell", None, None))
    return jax.shard_map(on_device, mesh=mesh, in_specs=in_specs, out_specs=P(None, "cell", "rank"), check_vma=False)
```

time: 50.8 us -> 44.8 us (0.88)
  Pallas kernels: 48.6 us -> 42.5 us
    pallas_call x1, Pallas kernels: 48.6 us -> 42.5 us  [on_device(): pl.pallas_call(kernel, out_shape=jax.ShapeDtypeStruct(factors.shape, f32)...]
where the time goes in v3:
time: 44.8 us; the launch traced here: 44.6 us
  Pallas kernels  42.5 us (95%)
  local copies, waits for them, and re-layouts  2.06 us (5%)
    pallas_call x1, Pallas kernels, on_device(): pl.pallas_call(kernel, out_shape=jax.ShapeDtypeStruct(factors.shape, f32)...  42.5 us
    unnamed x1, local copies, waits for them, and re-layouts  2.06 us

profile of v3, /device:TPU:1, one launch (start us, length us, event | category | flops | bytes accessed | tf_op | source)
XLA Modules:
  0.0 44.6 jit_solution(2877560672110888594)
XLA Ops:
  0.0 42.5 %shard_map.46 = f32[48,4,1024]{2,1,0:T(4,128)} custom-call(s32[2,3]{1,0:T(2,128)} %tri.1, f32[1,1024]{1,0:T(1,128)} %bitcast.1, f32[48,4,1024]{2,1,0:T(4,128)} %fac_hbm.1, bf16[2,4,256,256]{3,2,1,0:T(8,128)(2,1)} %tgt.1), custom_call_target="tpu_custom_call" | custom-call | tf_op jit(solution)/shard_map/pallas_call | solution.py:360
  42.6 2.1 %copy.6 = f32[48,4,1024]{2,1,0:T(4,128)} copy(f32[48,4,1024]{2,1,0:T(4,128)} %shard_map.46) | data formatting | bytes 1572864

commit v4 on v3

--- a/solution.py
+++ b/solution.py
@@ -136,17 +136,20 @@
     def first_wait(which, d):
         arrived(block(which, slice(None), (first_pos[which] + 4 - d) % 4, second_pos[which]), first_r.at[which * 3 + d - 1])
 
-    passed_on = {1: (0, 2), 0: (1, 3)}
+    def passed_on(h, e, up):
+        return (e, up) in (((0, 1), (1, 1), (3, 0)), ((0, 0), (1, 1), (3, 0)))[h]
 
     def near_sem(which, h, e, up):
-        return near_r.at[(which * 2 + h) * 5 + (e if e in passed_on[up] else 4)]
+        return near_r.at[(which * 2 + h) * 4 + ((0, 1, None, 2)[e] if passed_on(h, e, up) else 3)]
 
     def near(which, h, e):
         for up in (1, 0):
             send(which, h, first_pos[which] + e, second_pos[which], near_sem(which, h, e, up), along_second(which, 1 if up else 3))
+        if e == 2:
+            send(which, h, first_pos[which] + e, second_pos[which], far_r.at[which * 2 + h], along_second(which, 2))
 
     def forward(which, h, e):
-        up = 1 if e in passed_on[1] else 0
+        up = 1 if passed_on(h, e, 1) else 0
         p, q = first_pos[which] + e, second_pos[which] + (3 if up else 1)
         arrived(block(which, h, p % 4, q % 4), near_sem(which, h, e, up))
         send(which, h, p, q, far_r.at[which * 2 + h], along_second(which, 1 if up else 3))
@@ -178,7 +181,7 @@
             first_wait(which, d)
             near(which, 0, 4 - d)
             near(which, 1, 4 - d)
-    for e in (0, 1, 3, 2):
+    for e in (0, 1, 3):
         for which, h in both:
             forward(which, h, e)
 
@@ -186,9 +189,10 @@
         part = pl.ds(i, 2)
         return rcopy(pm_send.at[part], pm_recv.at[part], sent.at[2], pm_r.at[i // 2], other, zh)
 
+    five = scaled.at[0, pl.ds(0, 80)]
     for h in range(2):
         for which in range(2):
-            arrived(bfull.at[h, 0], near_r.at[(which * 2 + h) * 5 + 4])
+            arrived(five, near_r.at[(which * 2 + h) * 4 + 3])
             arrived(bfull.at[h, 0], far_r.at[which * 2 + h])
         bs = bfull[h].reshape(256, hw).astype(f32)
         cs = cfull[h].reshape(256, hw)
@@ -317,17 +321,20 @@
     steps = []
     for t in range(2):
         g = arecv[t]
-        steps.append((tri[t, 0], learn_rate * (w[...] * jnp.concatenate([g[0:4], g[4:8]], axis=1))))
+        step = [learn_rate * (w[...] * jnp.concatenate([g[0:4], g[4:8]], axis=1))]
         for which in range(2):
-            g = jnp.concatenate([sums[which, 0, t], sums[which, 1, t]], axis=1)
-            steps.append((tri[t, 1 + which], learn_rate * g))
+            step.append(learn_rate * jnp.concatenate([sums[which, 0, t], sums[which, 1, t]], axis=1))
+        steps.append(step)
 
     @pl.loop(0, 48)
     def _(attr):
-        step = jnp.zeros((4, rows), f32)
-        for which, g in steps:
-            step = step + jnp.where(which == attr, g, 0.0)
-        out[attr] = fac[attr] - step
+        value = fac[attr]
+        for t in range(2):
+            step = jnp.where(tri[t, 2] == attr, steps[t][2], 0.0)
+            for m in (1, 0):
+                step = jnp.where(tri[t, m] == attr, steps[t][m], step)
+            value = value - step
+        out[attr] = value
 
     def left(ref, k):
         rcopy(ref, ref, sent.at[k], sent.at[k], 0, 0).wait_send()
@@ -391,7 +398,7 @@
             V((2, 16, 16, 128), bf16),
             V((2, 8, hw), f32),
             V((2, 8, hw), f32),
-            dma((2,)), dma((2,)), dma((6,)), dma((3,)), dma((6,)), dma((20,)), dma((4,)), dma((4,)), dma((4,)), dma((4,)),
+            dma((2,)), dma((2,)), dma((6,)), dma((3,)), dma((6,)), dma((16,)), dma((4,)), dma((4,)), dma((4,)), dma((4,)),
         ],
         compiler_params=pltpu.CompilerParams(collective_id=0, has_side_effects=True, vmem_limit_bytes=56 * 1024 * 1024),
     )(triples, rank_weights.reshape(1, rows), factors, targets)

time: 44.8 us -> 44.4 us (level)
  no operation moved by 1% of the time
where the time goes in v4:
time: 44.4 us; the launch traced here: 44.2 us
  Pallas kernels  42.1 us (95%)
  local copies, waits for them, and re-layouts  2.06 us (5%)
    pallas_call x1, Pallas kernels, on_device(): pl.pallas_call(kernel, out_shape=jax.ShapeDtypeStruct(factors.shape, f32)...  42.1 us
    unnamed x1, local copies, waits for them, and re-layouts  2.06 us

profile of v4, /device:TPU:1, one launch (start us, length us, event | category | flops | bytes accessed | tf_op | source)
XLA Modules:
  0.0 44.2 jit_solution(921069291337830965)
XLA Ops:
  0.0 42.1 %shard_map.46 = f32[48,4,1024]{2,1,0:T(4,128)} custom-call(s32[2,3]{1,0:T(2,128)} %tri.1, f32[1,1024]{1,0:T(1,128)} %bitcast.1, f32[48,4,1024]{2,1,0:T(4,128)} %fac_hbm.1, bf16[2,4,256,256]{3,2,1,0:T(8,128)(2,1)} %tgt.1), custom_call_target="tpu_custom_call" | custom-call | tf_op jit(solution)/shard_map/pallas_call | solution.py:367
  42.1 2.1 %copy.6 = f32[48,4,1024]{2,1,0:T(4,128)} copy(f32[48,4,1024]{2,1,0:T(4,128)} %shard_map.46) | data formatting | bytes 1572864

commit v5 on v4

--- a/solution.py
+++ b/solution.py
@@ -29,7 +29,7 @@
     return pl.when(jnp.logical_not(flag))
 
 
-def kernel(tri, w, fac_hbm, tgt, out, fac, msg, amsg, col, acol, bfull, cfull, wa, tg, scaled, pm_own, pm_send, pm_recv,
+def kernel(tri, w, fac_hbm, tgt, steps, fac, msg, amsg, col, acol, bfull, cfull, wa, tg, scaled, pm_own, pm_send, pm_recv,
            resid, resid_t, ga, gb, gc, gb_send, gc_send, b1, c1, b2_send, c2_send, b2, c2, asend, arecv,
            l_sem, t_sem, sent, col_r, first_r, near_r, far_r, pm_r, r_r, f_r):
     cell = lax.axis_index("cell")
@@ -94,7 +94,6 @@
                 @unless(is_self)
                 def _():
                     col_copy(t, dl).start()
-                    acol_copy(t).start()
 
                 @pl.when(is_self)
                 def _():
@@ -160,6 +159,10 @@
             first(which, d)
     for which, h in both:
         near(which, h, 0)
+    for t in range(2):
+        @unless((core == zh) & (zh == t))
+        def _():
+            acol_copy(t).start()
 
     tg_copy = rcopy(tgt.at[zh], tg.at[pl.ds(core * 4, 4)], t_sem.at[0], t_sem.at[1], other, zh)
     tg_copy.start()
@@ -318,23 +321,11 @@
         for t in range(2):
             total = sum(buf_r[h, 2 * k + t].astype(f32) for k in range(8))
             sums[which, h, t] = jnp.concatenate([total[4 * q:4 * q + 4] for q in range(4)], axis=1)
-    steps = []
     for t in range(2):
         g = arecv[t]
-        step = [learn_rate * (w[...] * jnp.concatenate([g[0:4], g[4:8]], axis=1))]
+        steps[3 * t] = learn_rate * (w[...] * jnp.concatenate([g[0:4], g[4:8]], axis=1))
         for which in range(2):
-            step.append(learn_rate * jnp.concatenate([sums[which, 0, t], sums[which, 1, t]], axis=1))
-        steps.append(step)
-
-    @pl.loop(0, 48)
-    def _(attr):
-        value = fac[attr]
-        for t in range(2):
-            step = jnp.where(tri[t, 2] == attr, steps[t][2], 0.0)
-            for m in (1, 0):
-                step = jnp.where(tri[t, m] == attr, steps[t][m], step)
-            value = value - step
-        out[attr] = value
+            steps[3 * t + 1 + which] = learn_rate * jnp.concatenate([sums[which, 0, t], sums[which, 1, t]], axis=1)
 
     def left(ref, k):
         rcopy(ref, ref, sent.at[k], sent.at[k], 0, 0).wait_send()
@@ -355,6 +346,24 @@
         left(scaled.at[0, pl.ds(0, 64)], 0)
         left(asend.at[0], 4)
         left(scaled.at[0, pl.ds(0, 240)], 5)
+
+
+def update_kernel(tri, fac, steps, out):
+    out[...] = fac[...]
+    for t in range(2):
+        for m in range(3):
+            out[tri[t, m]] -= steps[3 * t + m]
+
+
+def update(factors, triples, steps):
+    vmem = pl.BlockSpec(memory_space=pltpu.VMEM)
+    return pl.pallas_call(
+        update_kernel,
+        out_shape=jax.ShapeDtypeStruct(factors.shape, f32),
+        in_specs=[pl.BlockSpec(memory_space=pltpu.SMEM), vmem, vmem],
+        out_specs=vmem,
+        compiler_params=pltpu.CompilerParams(vmem_limit_bytes=8 * 1024 * 1024),
+    )(triples, factors, steps)
 
 
 def on_device(factors, rank_weights, triples, targets):
@@ -364,9 +373,9 @@
     hbm = pl.BlockSpec(memory_space=pl.ANY)
     dma = pltpu.SemaphoreType.DMA
     V = pltpu.VMEM
-    return pl.pallas_call(
+    steps = pl.pallas_call(
         kernel,
-        out_shape=jax.ShapeDtypeStruct(factors.shape, f32),
+        out_shape=jax.ShapeDtypeStruct((6,) + factors.shape[1:], f32),
         in_specs=[pl.BlockSpec(memory_space=pltpu.SMEM), vmem, hbm, hbm],
         out_specs=vmem,
         scratch_shapes=[
@@ -400,8 +409,9 @@
             V((2, 8, hw), f32),
             dma((2,)), dma((2,)), dma((6,)), dma((3,)), dma((6,)), dma((16,)), dma((4,)), dma((4,)), dma((4,)), dma((4,)),
         ],
-        compiler_params=pltpu.CompilerParams(collective_id=0, has_side_effects=True, vmem_limit_bytes=56 * 1024 * 1024),
+        compiler_params=pltpu.CompilerParams(collective_id=0, has_side_effects=True, vmem_limit_bytes=62 * 1024 * 1024),
     )(triples, rank_weights.reshape(1, rows), factors, targets)
+    return update(factors, triples, steps)
 
 
 def solution(mesh):

time: 44.4 us -> 43.4 us (0.977)
  local copies, waits for them, and re-layouts: 2.06 us -> 0.89 us
    unnamed x1 -> x6, local copies, waits for them, and re-layouts: 2.06 us -> 0.89 us
    pallas_call x1 -> x2, Pallas kernels: 42.1 us -> 42.3 us  [the longest x1 40.8 us: on_device(): pl.pallas_call(kernel, out_shape=jax.ShapeDtypeStruct((6,) + factors.shap...]
where the time goes in v5:
time: 43.4 us; the launch traced here: 43.3 us
  Pallas kernels  42.3 us (97%)
  local copies, waits for them, and re-layouts  0.89 us (2%)
    pallas_call x1, Pallas kernels, on_device(): pl.pallas_call(kernel, out_shape=jax.ShapeDtypeStruct((6,) + factors.shap...  40.8 us
    pallas_call x1, Pallas kernels, update(): pl.pallas_call(update_kernel, out_shape=jax.ShapeDtypeStruct(factors.shap...  1.5 us
    unnamed x6, local copies, waits for them, and re-layouts  0.89 us

profile of v5, /device:TPU:1, one launch (start us, length us, event | category | flops | bytes accessed | tf_op | source)
XLA Modules:
  0.0 43.3 jit_solution(11447680070253342830)
XLA Ops:
  0.0 0.0 copy-start
  0.0 0.0 copy-start.2
  0.0 40.8 %shard_map.46.steps = f32[6,4,1024]{2,1,0:T(4,128)} custom-call(s32[2,3]{1,0:T(2,128)} %tri.3, f32[1,1024]{1,0:T(1,128)} %bitcast.1, f32[48,4,1024]{2,1,0:T(4,128)} %fac.1, bf16[2,4,256,256]{3,2,1,0:T(8,128)(2,1)} %tgt.1), custom_call_target="tpu_custom_call" | custom-call | tf_op jit(solution)/shard_map/pallas_call | solution.py:376
  40.9 0.0 copy-done
  40.9 0.0 copy-done.2
  40.9 0.0 copy-start.1
  40.9 0.9 %copy-done.1 = f32[6,4,1024]{2,1,0:T(4,128)S(1)} copy-done((f32[6,4,1024]{2,1,0:T(4,128)S(1)}, f32[6,4,1024]{2,1,0:T(4,128)}, u32[]{:S(2)}) %copy-start.1) | copy-done | bytes 98328
  41.8 1.5 %shard_map.47 = f32[48,4,1024]{2,1,0:T(4,128)} custom-call(s32[2,3]{1,0:T(2,128)S(1)} %copy-done.2, f32[48,4,1024]{2,1,0:T(4,128)S(1)} %copy-done, f32[6,4,1024]{2,1,0:T(4,128)S(1)} %copy-done.1), custom_call_target="tpu_custom_call" | custom-call | tf_op jit(solution)/shard_map/pallas_call | solution.py:360
Async XLA Ops:
  0.0 40.9 %copy-start = (f32[48,4,1024]{2,1,0:T(4,128)S(1)}, f32[48,4,1024]{2,1,0:T(4,128)}, u32[]{:S(2)}) copy-start(f32[48,4,1024]{2,1,0:T(4,128)} %fac.1) | copy-start | bytes 2359300
  0.0 40.9 %copy-start.2 = (s32[2,3]{1,0:T(2,128)S(1)}, s32[2,3]{1,0:T(2,128)}, u32[]{:S(2)}) copy-start(s32[2,3]{1,0:T(2,128)} %tri.3) | copy-start | bytes 76
  40.9 0.9 %copy-start.1 = (f32[6,4,1024]{2,1,0:T(4,128)S(1)}, f32[6,4,1024]{2,1,0:T(4,128)}, u32[]{:S(2)}) copy-start(f32[6,4,1024]{2,1,0:T(4,128)} %shard_map.46.steps) | copy-start | bytes 294916

commit v6 on v0

v6 whole, which is shorter than its diff:
```python
import jax
import jax.numpy as jnp
from jax import lax
from jax.experimental import pallas as pl
from jax.experimental.pallas import tpu as pltpu
from jax.sharding import PartitionSpec as P

learn_rate = 0.02
MESH = pl.DeviceIdType.MESH
f32, bf16 = jnp.float32, jnp.bfloat16
NT = (((1,), (1,)), ((), ()))


def cell_of(x, y, zl, core):
    return ((x * 4 + y) * 2 + zl) * 2 + core


def rcopy(src, dst, send_sem, recv_sem, cell, rank):
    return pltpu.make_async_remote_copy(
        src_ref=src, dst_ref=dst, send_sem=send_sem, recv_sem=recv_sem,
        device_id={"cell": cell, "rank": rank}, device_id_type=MESH)


def arrived(ref, sem):
    rcopy(ref, ref, sem, sem, 0, 0).wait_recv()


def unless(flag):
    return pl.when(jnp.logical_not(flag))


def kernel(tri, w, fac_hbm, tgt, steps, fac, bmsg, cmsg, amsg, bcol, ccol, acol, bfull, cfull, wa, tg, tgh, scaled, pm,
           resid, resid_t, ga, gb, gc, gb_send, gc_send, gx_send, gx, b1, c1, b2_send, c2_send, b2, c2, asend, arecv,
           l_sem, t_sem, sent, col_r, first_r, second_r, cx_r, gx_r, r_r, f_r):
    cell = lax.axis_index("cell")
    zh = lax.axis_index("rank")
    core = cell % 2
    zl = (cell // 2) % 2
    y = (cell // 4) % 4
    x = cell // 16
    rows = w.shape[1]
    hw = rows // 2
    other = cell_of(x, y, zl, 1 - core)

    load = pltpu.make_async_copy(fac_hbm, fac, l_sem.at[0])
    load.start()
    own_tgt = pltpu.make_async_copy(tgt.at[zh], tg.at[pl.ds(core * 4, 4)], l_sem.at[1])
    own_tgt.start()

    barrier = pltpu.get_barrier_semaphore()

    def greet(to, rank):
        pl.semaphore_signal(barrier, inc=1, device_id={"cell": to, "rank": rank}, device_id_type=MESH)

    for k in range(1, 8):
        greet(cell_of(x, y, (zl + k // 4) % 2, (core + k // 2) % 2), (zh + k) % 2)
    for d in range(1, 4):
        greet(cell_of((x + d) % 4, y, zl, core), zh)
        greet(cell_of(x, (y + d) % 4, zl, core), zh)

    load.wait()
    for t in range(2):
        a = w[...] * fac[tri[t, 0]]
        b = fac[tri[t, 1]]
        c = fac[tri[t, 2]]
        bmsg[t] = jnp.concatenate([b[:, 256 * q:256 * q + 256] for q in range(4)], axis=0).astype(bf16)
        cmsg[t] = jnp.concatenate([c[:, 256 * q:256 * q + 256] for q in range(4)], axis=0).astype(bf16)
        amsg[t] = jnp.concatenate([a[:, :hw], a[:, hw:]], axis=0)
    pl.semaphore_wait(barrier, 13)

    def col_b(t, dl):
        return rcopy(bmsg.at[t], bcol.at[core * 2 + zh], sent.at[0], col_r.at[0], cell_of(x, y, (zl + dl) % 2, zl), t)

    def col_c(t, dl):
        return rcopy(cmsg.at[t], ccol.at[zl * 2 + core], sent.at[1], col_r.at[1], cell_of(x, y, (zl + dl) % 2, zh), t)

    def col_a(t, dc):
        return rcopy(amsg.at[t], acol.at[core * 2 + zh], sent.at[2], col_r.at[2], cell_of(x, y, zl, (core + dc) % 2), t)

    for t in range(2):
        c_self = (core == zh) & (zh == t)
        b_self = (core == zl) & (zh == t)

        @unless(c_self)
        def _():
            col_c(t, 0).start()

        @pl.when(c_self)
        def _():
            ccol[zl * 2 + core] = cmsg[t]

        @unless(b_self)
        def _():
            col_b(t, 0).start()

        @pl.when(b_self)
        def _():
            bcol[core * 2 + zh] = bmsg[t]

    def arrived_some(flag, ref, n, sem):
        @unless(flag)
        def _():
            arrived(ref, sem)

        @pl.when(flag)
        def _():
            arrived(ref.at[pl.ds(0, n)], sem)

    for t in range(2):
        col_c(t, 1).start()
        col_b(t, 1).start()
    arrived_some(core == zh, ccol, 3, col_r.at[1])
    got = [ccol[k].astype(f32) for k in range(4)]
    for h in range(2):
        cfull[core, h, x, y] = jnp.concatenate(
            [jnp.concatenate([m[4 * q:4 * q + 4] for m in got], axis=0) for q in (2 * h, 2 * h + 1)], axis=1).astype(bf16)

    def x_first(which, h):
        return which == h

    def first_pos(which, h):
        return x if x_first(which, h) else y

    def second_pos(which, h):
        return y if x_first(which, h) else x

    def block(which, h, p, q):
        bx, by = (p, q) if x_first(which, h) else (q, p)
        return bfull.at[h, bx, by] if which == 0 else cfull.at[core, h, bx, by]

    def along(along_x, d, l=zl, c=core):
        return cell_of((x + d) % 4, y, l, c) if along_x else cell_of(x, (y + d) % 4, l, c)

    def send(which, h, p, q, recv_sem, to):
        view = block(which, h, p % 4, q % 4)
        rcopy(view, view, sent.at[3], recv_sem, to, zh).start()

    def first_sem(which, h, d):
        return first_r.at[(which * 2 + h) * 3 + d - 1]

    def first(which, h, d):
        send(which, h, first_pos(which, h), second_pos(which, h), first_sem(which, h, d), along(x_first(which, h), d))

    def first_wait(which, h, d):
        arrived(block(which, h, (first_pos(which, h) + 4 - d) % 4, second_pos(which, h)), first_sem(which, h, d))

    def second(which, h, e):
        for d in (2, 1, 3):
            send(which, h, first_pos(which, h) + e, second_pos(which, h), second_r.at[which * 2 + h],
                 along(not x_first(which, h), d))

    def second_wait(which, h):
        arrived(scaled.at[0, 0, pl.ds(0, 192)], second_r.at[which * 2 + h])

    both = [(which, h) for which in (1, 0) for h in range(2)]
    for h in range(2):
        for d in (2, 1, 3):
            first(1, h, d)
    arrived_some(core == zl, bcol, 3, col_r.at[0])
    got = [bcol[2 * (k % 2) + k // 2].astype(f32) for k in range(4)]
    for h in range(2):
        bfull[h, x, y] = jnp.concatenate(
            [jnp.concatenate([m[4 * q:4 * q + 4] for m in got], axis=0) for q in (2 * h, 2 * h + 1)], axis=1).astype(bf16)
        for d in (2, 1, 3):
            first(0, h, d)
    for which, h in both:
        second(which, h, 0)

    for t in range(2):
        col_a(t, 1).start()
        a_self = zh == t

        @unless(a_self)
        def _():
            col_a(t, 0).start()

        @pl.when(a_self)
        def _():
            acol[core * 2 + zh] = amsg[t]
    tg_copy = rcopy(tgt.at[zh], tg.at[pl.ds(core * 4, 4)], t_sem.at[0], t_sem.at[1], other, zh)
    tg_copy.start()

    for which in (1, 0):
        for d in (1, 3, 2):
            for h in range(2):
                first_wait(which, h, d)
                second(which, h, 4 - d)
    arrived(acol.at[pl.ds(0, 3)], col_r.at[2])
    for rh in range(2):
        got = [acol[c * 2 + rh] for c in range(2)]
        for h in range(2):
            wa[rh, :, h * hw:(h + 1) * hw] = jnp.concatenate([m[4 * h:4 * h + 4] for m in got], axis=0)
    own_tgt.wait()
    arrived(tg.at[pl.ds((1 - core) * 4, 4)], t_sem.at[1])
    for i in range(8):
        parts = tg[i].astype(f32).reshape(16, 2, 8, 256)
        tgh[i * 128:(i + 1) * 128, :] = jnp.where(core == 0, parts[:, 0], parts[:, 1]).reshape(128, 256)

    def c_copy(h):
        return rcopy(cfull.at[core, h], cfull.at[core, h], sent.at[4], cx_r.at[h], other, zh)

    for h in range(2):
        second_wait(1, h)
        c_copy(h).start()

    def b_part(h, rh, lanes):
        parts = bfull[h, :, :, :, lanes].astype(f32).reshape(16, 2, 8, -1)
        return jnp.where(rh == 0, parts[:, 0], parts[:, 1]).reshape(128, -1)

    for rh, halves in ((core, (0,)), (core, (1,)), (1 - core, (0, 1))):
        if len(halves) == 1:
            second_wait(0, halves[0])
        else:
            for h in halves:
                arrived(cfull.at[rh, h], cx_r.at[h])
        bs = [b_part(h, rh, slice(0, hw)) for h in halves]
        cs = [cfull[rh, h].reshape(256, hw) for h in halves]
        for i in range(0, 8, 2):
            part = None
            at = slice(i * 128, (i + 2) * 128)
            for n, h in enumerate(halves):
                s = jnp.concatenate(
                    [wa[rh, k:k + 1, h * hw:(h + 1) * hw] * bs[n] for k in (i, i + 1)], axis=0).astype(bf16)
                scaled[rh, h, at, :] = s
                term = lax.dot_general(s, cs[n], NT, preferred_element_type=f32)
                part = term if part is None else part + term
            if halves == (0,):
                pm[at, :] = part
            elif halves == (1,):
                pm[at, :] += part
            else:
                r = (pm[at, :] + part - tgh[at, :]).astype(bf16)
                resid[at, :] = r
                resid_t[:, at] = r.T

    def scatter(which, h, q):
        src, dst = ((gb_send, b1), (gc_send, c1))[which]
        on_x = not x_first(which, h)
        for d in (2, 1, 3):
            view = src.at[h, q, (x + d) % 4] if on_x else src.at[h, q, :, (y + d) % 4]
            rcopy(view, dst.at[h, d - 1, q], sent.at[6], r_r.at[which * 2 + h], along(on_x, d), zh).start()

    def grad_b(h, q):
        lanes = slice(q * 256, (q + 1) * 256)
        wlanes = slice(h * hw + q * 256, h * hw + (q + 1) * 256)
        accs = []
        for rh in range(2):
            cs = cfull[rh, h, :, :, :, lanes].reshape(256, 256)
            bs = bfull[h, :, :, :, lanes].astype(f32).reshape(16, 2, 8, 256)[:, rh].reshape(128, 256)
            acc = jnp.zeros((128, 256), f32)
            for i in range(0, 8, 2):
                xprod = jnp.dot(resid[i * 128:(i + 2) * 128, :], cs, preferred_element_type=f32)
                for k in range(2):
                    xp = xprod[k * 128:(k + 1) * 128]
                    ga[rh, i + k:i + k + 1, wlanes] = jnp.sum(xp * bs, axis=0, keepdims=True)
                    acc = acc + wa[rh, i + k:i + k + 1, wlanes] * xp
            accs.append(acc.reshape(16, 1, 8, 256))
        part = jnp.concatenate(accs, axis=1).reshape(4, 4, 16, 256)
        gb[h, q] = part
        gb_send[h, q] = part.astype(bf16)
        scatter(0, h, q)

    def grad_c_other(h):
        gx_send[h] = jnp.dot(resid_t[...], scaled[1 - core, h], preferred_element_type=f32).astype(bf16)
        rcopy(gx_send.at[h], gx.at[h], sent.at[5], gx_r.at[h], other, zh).start()

    def grad_c(h):
        part = jnp.dot(resid_t[...], scaled[core, h], preferred_element_type=f32)
        arrived(gx.at[h], gx_r.at[h])
        for q in range(2):
            lanes = slice(q * 256, (q + 1) * 256)
            total = (part[:, lanes] + gx[h, :, lanes].astype(f32)).reshape(4, 4, 16, 256)
            gc[h, q] = total
            gc_send[h, q] = total.astype(bf16)
            scatter(1, h, q)

    grad_b(0, 0)
    grad_b(1, 0)
    grad_c_other(0)
    grad_c_other(1)
    grad_b(0, 1)
    grad_b(1, 1)
    grad_c(0)
    grad_c(1)

    def a_copy(k):
        return rcopy(asend.at[k], arecv.at[zh * 2 + core], sent.at[9], col_r.at[3], cell_of(x, y, zl, k % 2), k // 2)

    for k in range(4):
        g = ga[k // 2, 4 * (k % 2):4 * (k % 2) + 4, :]
        asend[k] = jnp.concatenate([g[:, :hw], g[:, hw:]], axis=0)
        is_self = (core == k % 2) & (zh == k // 2)

        @unless(is_self)
        def _():
            a_copy(k).start()

        @pl.when(is_self)
        def _():
            arecv[zh * 2 + core] = asend[k]

    bufs = ((b2_send, b2), (c2_send, c2))

    def final_copy(which, h, d, s):
        buf_s, buf_r = bufs[which]
        p = first_pos(which, h)
        if which == 0:
            to, rank = along(x_first(which, h), d, core, s % 2), s // 2
        else:
            to, rank = along(x_first(which, h), d, s // 2, s % 2), core
        return rcopy(buf_s.at[h, (p + d) % 4, s], buf_r.at[h, (p * 2 + zl) * 2 + zh], sent.at[7 + which],
                     f_r.at[which * 2 + h], to, rank)

    def final_self(which, s):
        if which == 0:
            return (core == zl) & (core == s % 2) & (zh == s // 2)
        return (zl == s // 2) & (core == s % 2) & (zh == core)

    order = [(0, 0), (0, 1), (1, 1), (1, 0)]
    for which, h in order:
        buf, g = ((b1, gb), (c1, gc))[which]
        mine = g[h, :, x] if not x_first(which, h) else g[h, :, :, y]
        arrived(buf.at[h], r_r.at[which * 2 + h])
        total = mine + buf[h, 0].astype(f32) + buf[h, 1].astype(f32) + buf[h, 2].astype(f32)
        buf_s, buf_r = bufs[which]
        for p in range(4):
            for s in range(4):
                buf_s[h, p, s] = jnp.concatenate(
                    [total[q // 2, p, 4 * s:4 * s + 4, 128 * (q % 2):128 * (q % 2) + 128] for q in range(4)],
                    axis=0).astype(bf16)
        for d in (2, 1, 3):
            for s in range(4):
                final_copy(which, h, d, s).start()
        for s in range(4):
            @unless(final_self(which, s))
            def _():
                final_copy(which, h, 0, s).start()

            @pl.when(final_self(which, s))
            def _():
                buf_r[h, (first_pos(which, h) * 2 + zl) * 2 + zh] = buf_s[h, first_pos(which, h), s]

    arrived(arecv.at[pl.ds(0, 3)], col_r.at[3])
    for t in range(2):
        g = arecv[2 * t] + arecv[2 * t + 1]
        steps[3 * t] = learn_rate * (w[...] * jnp.concatenate([g[0:4], g[4:8]], axis=1))
    for which, h in order:
        buf_r = bufs[which][1]
        arrived_some(core == (zl, zh)[which], buf_r.at[h], 15, f_r.at[which * 2 + h])
        for t in range(2):
            total = sum(buf_r[h, 2 * k + t].astype(f32) for k in range(8))
            steps[3 * t + 1 + which, :, h * hw:(h + 1) * hw] = learn_rate * jnp.concatenate(
                [total[4 * q:4 * q + 4] for q in range(4)], axis=1)

    def left(n, k):
        ref = pm.at[pl.ds(0, n)]
        rcopy(ref, ref, sent.at[k], sent.at[k], 0, 0).wait_send()

    def left_some(flag, n, fewer, k):
        @unless(flag)
        def _():
            left(n, k)

        @pl.when(flag)
        def _():
            left(fewer, k)

    tg_copy.wait_send()
    left_some(core == zl, 32, 24, 0)
    left_some(core == zh, 32, 24, 1)
    left(48, 2)
    left(960, 3)
    left(512, 4)
    left(512, 5)
    left(768, 6)
    left_some(core == zl, 128, 120, 7)
    left_some(core == zh, 128, 120, 8)
    left(48, 9)


def update_kernel(tri, fac, steps, out):
    out[...] = fac[...]
    for t in range(2):
        for m in range(3):
            out[tri[t, m]] -= steps[3 * t + m]


def update(factors, triples, steps):
    vmem = pl.BlockSpec(memory_space=pltpu.VMEM)
    return pl.pallas_call(
        update_kernel,
        out_shape=jax.ShapeDtypeStruct(factors.shape, f32),
        in_specs=[pl.BlockSpec(memory_space=pltpu.SMEM), vmem, vmem],
        out_specs=vmem,
        compiler_params=pltpu.CompilerParams(vmem_limit_bytes=8 * 1024 * 1024),
    )(triples, factors, steps)


def on_device(factors, rank_weights, triples, targets):
    rows = rank_weights.shape[0]
    hw = rows // 2
    vmem = pl.BlockSpec(memory_space=pltpu.VMEM)
    hbm = pl.BlockSpec(memory_space=pl.ANY)
    dma = pltpu.SemaphoreType.DMA
    V = pltpu.VMEM
    steps = pl.pallas_call(
        kernel,
        out_shape=jax.ShapeDtypeStruct((6,) + factors.shape[1:], f32),
        in_specs=[pl.BlockSpec(memory_space=pltpu.SMEM), vmem, hbm, hbm],
        out_specs=vmem,
        scratch_shapes=[
            V(factors.shape, f32),
            V((2, 16, 256), bf16),
            V((2, 16, 256), bf16),
            V((2, 8, hw), f32),
            V((4, 16, 256), bf16),
            V((4, 16, 256), bf16),
            V((4, 8, hw), f32),
            V((2, 4, 4, 16, hw), bf16),
            V((2, 2, 4, 4, 16, hw), bf16),
            V((2, 8, rows), f32),
            V((8, 256, 256), bf16),
            V((1024, 256), f32),
            V((2, 2, 1024, hw), bf16),
            V((1024, 256), f32),
            V((1024, 256), bf16),
            V((256, 1024), bf16),
            V((2, 8, rows), f32),
            V((2, 2, 4, 4, 16, 256), f32),
            V((2, 2, 4, 4, 16, 256), f32),
            V((2, 2, 4, 4, 16, 256), bf16),
            V((2, 2, 4, 4, 16, 256), bf16),
            V((2, 256, hw), bf16),
            V((2, 256, hw), bf16),
            V((2, 3, 2, 4, 16, 256), bf16),
            V((2, 3, 2, 4, 16, 256), bf16),
            V((2, 4, 4, 16, 128), bf16),
            V((2, 4, 4, 16, 128), bf16),
            V((2, 16, 16, 128), bf16),
            V((2, 16, 16, 128), bf16),
            V((4, 8, hw), f32),
            V((4, 8, hw), f32),
            dma((2,)), dma((2,)), dma((10,)), dma((4,)), dma((12,)), dma((4,)), dma((2,)), dma((2,)), dma((4,)), dma((4,)),
        ],
        compiler_params=pltpu.CompilerParams(collective_id=0, has_side_effects=True, vmem_limit_bytes=62 * 1024 * 1024),
    )(triples, rank_weights.reshape(1, rows), factors, targets)
    return update(factors, triples, steps)


def solution(mesh):
    in_specs = (P(None, "cell", "rank"), P("rank"), P(), P(None, "cell", None, None))
    return jax.shard_map(on_device, mesh=mesh, in_specs=in_specs, out_specs=P(None, "cell", "rank"), check_vma=False)
```

time: 890 us -> 40.6 us (0.05)
  waiting for transfers between devices: 824 us -> 0 us
  Pallas kernels: 0 us -> 39.5 us
  between operations: 25.1 us -> 0.03 us
  local copies, waits for them, and re-layouts: 18.4 us -> 0.89 us
  other arithmetic: 14.4 us -> 0 us
    unnamed x5 -> x0, waiting for transfers between devices: 553 us -> none
    all_gather x2 -> x0, waiting for transfers between devices: 203 us -> none  [on_device(): lax.all_gather(jnp.stack([factors[second_attr], factors[third_attr]]), 'c...]
    psum x1 -> x0, waiting for transfers between devices: 67.7 us -> none  [on_device(): model = lax.psum(partial_model, 'rank')]
    pallas_call x0 -> x2, Pallas kernels: none -> 39.5 us  [the longest x1 38 us: on_device(): pl.pallas_call(kernel, out_shape=jax.ShapeDtypeStruct((6,) + factors.shap...]
    slice x6 -> x0, local copies, waits for them, and re-layouts: 10.6 us -> none  [the longest x2 4.62 us: on_device(): full_second = gathered[0]]
  transfers between devices with their start and end apart: 4 -> 0, of which waited for: 4 -> 0; matrix products, arithmetic and copies ran while one was open for 1% -> 0% of each run, Pallas kernels for 0% -> 0%
where the time goes in v6:
time: 40.6 us; the launch traced here: 40.4 us
  Pallas kernels  39.5 us (97%)
  local copies, waits for them, and re-layouts  0.89 us (2%)
    pallas_call x1, Pallas kernels, on_device(): pl.pallas_call(kernel, out_shape=jax.ShapeDtypeStruct((6,) + factors.shap...  38 us
    pallas_call x1, Pallas kernels, update(): pl.pallas_call(update_kernel, out_shape=jax.ShapeDtypeStruct(factors.shap...  1.5 us
    unnamed x6, local copies, waits for them, and re-layouts  0.89 us

profile of v6, /device:TPU:1, one launch (start us, length us, event | category | flops | bytes accessed | tf_op | source)
XLA Modules:
  0.0 40.4 jit_solution(220855814847750677)
XLA Ops:
  0.0 0.0 copy-start
  0.0 0.0 copy-start.2
  0.0 38.0 %shard_map.46.steps = f32[6,4,1024]{2,1,0:T(4,128)} custom-call(s32[2,3]{1,0:T(2,128)} %tri.3, f32[1,1024]{1,0:T(1,128)} %bitcast.1, f32[48,4,1024]{2,1,0:T(4,128)} %fac.1, bf16[2,4,256,256]{3,2,1,0:T(8,128)(2,1)} %tgt.1), custom_call_target="tpu_custom_call" | custom-call | tf_op jit(solution)/shard_map/pallas_call | solution.py:406
  38.0 0.0 copy-done
  38.0 0.0 copy-done.2
  38.0 0.0 copy-start.1
  38.1 0.9 %copy-done.1 = f32[6,4,1024]{2,1,0:T(4,128)S(1)} copy-done((f32[6,4,1024]{2,1,0:T(4,128)S(1)}, f32[6,4,1024]{2,1,0:T(4,128)}, u32[]{:S(2)}) %copy-start.1) | copy-done | bytes 98328
  38.9 1.5 %shard_map.47 = f32[48,4,1024]{2,1,0:T(4,128)} custom-call(s32[2,3]{1,0:T(2,128)S(1)} %copy-done.2, f32[48,4,1024]{2,1,0:T(4,128)S(1)} %copy-done, f32[6,4,1024]{2,1,0:T(4,128)S(1)} %copy-done.1), custom_call_target="tpu_custom_call" | custom-call | tf_op jit(solution)/shard_map/pallas_call | solution.py:390
Async XLA Ops:
  0.0 38.0 %copy-start = (f32[48,4,1024]{2,1,0:T(4,128)S(1)}, f32[48,4,1024]{2,1,0:T(4,128)}, u32[]{:S(2)}) copy-start(f32[48,4,1024]{2,1,0:T(4,128)} %fac.1) | copy-start | bytes 2359300
  0.0 38.0 %copy-start.2 = (s32[2,3]{1,0:T(2,128)S(1)}, s32[2,3]{1,0:T(2,128)}, u32[]{:S(2)}) copy-start(s32[2,3]{1,0:T(2,128)} %tri.3) | copy-start | bytes 76
  38.0 0.9 %copy-start.1 = (f32[6,4,1024]{2,1,0:T(4,128)S(1)}, f32[6,4,1024]{2,1,0:T(4,128)}, u32[]{:S(2)}) copy-start(f32[6,4,1024]{2,1,0:T(4,128)} %shard_map.46.steps) | copy-start | bytes 294916

commit v7 on v6

--- a/solution.py
+++ b/solution.py
@@ -276,12 +276,12 @@
 
     grad_b(0, 0)
     grad_b(1, 0)
+    grad_c_other(1)
     grad_c_other(0)
-    grad_c_other(1)
     grad_b(0, 1)
     grad_b(1, 1)
+    grad_c(1)
     grad_c(0)
-    grad_c(1)
 
     def a_copy(k):
         return rcopy(asend.at[k], arecv.at[zh * 2 + core], sent.at[9], col_r.at[3], cell_of(x, y, zl, k % 2), k // 2)

time: 40.6 us -> 40.9 us (level)
  no operation moved by 1% of the time
where the time goes in v7:
time: 40.9 us; the launch traced here: 40.7 us
  Pallas kernels  39.8 us (97%)
  local copies, waits for them, and re-layouts  0.89 us (2%)
    pallas_call x1, Pallas kernels, on_device(): pl.pallas_call(kernel, out_shape=jax.ShapeDtypeStruct((6,) + factors.shap...  38.3 us
    pallas_call x1, Pallas kernels, update(): pl.pallas_call(update_kernel, out_shape=jax.ShapeDtypeStruct(factors.shap...  1.5 us
    unnamed x6, local copies, waits for them, and re-layouts  0.89 us

profile of v7, /device:TPU:1, one launch (start us, length us, event | category | flops | bytes accessed | tf_op | source)
XLA Modules:
  0.0 40.7 jit_solution(4231968814930172466)
XLA Ops:
  0.0 0.0 copy-start
  0.0 0.0 copy-start.2
  0.0 38.3 %shard_map.46.steps = f32[6,4,1024]{2,1,0:T(4,128)} custom-call(s32[2,3]{1,0:T(2,128)} %tri.3, f32[1,1024]{1,0:T(1,128)} %bitcast.1, f32[48,4,1024]{2,1,0:T(4,128)} %fac.1, bf16[2,4,256,256]{3,2,1,0:T(8,128)(2,1)} %tgt.1), custom_call_target="tpu_custom_call" | custom-call | tf_op jit(solution)/shard_map/pallas_call | solution.py:406
  38.3 0.0 copy-done
  38.3 0.0 copy-done.2
  38.3 0.0 copy-start.1
  38.3 0.9 %copy-done.1 = f32[6,4,1024]{2,1,0:T(4,128)S(1)} copy-done((f32[6,4,1024]{2,1,0:T(4,128)S(1)}, f32[6,4,1024]{2,1,0:T(4,128)}, u32[]{:S(2)}) %copy-start.1) | copy-done | bytes 98328
  39.2 1.5 %shard_map.47 = f32[48,4,1024]{2,1,0:T(4,128)} custom-call(s32[2,3]{1,0:T(2,128)S(1)} %copy-done.2, f32[48,4,1024]{2,1,0:T(4,128)S(1)} %copy-done, f32[6,4,1024]{2,1,0:T(4,128)S(1)} %copy-done.1), custom_call_target="tpu_custom_call" | custom-call | tf_op jit(solution)/shard_map/pallas_call | solution.py:390
Async XLA Ops:
  0.0 38.3 %copy-start = (f32[48,4,1024]{2,1,0:T(4,128)S(1)}, f32[48,4,1024]{2,1,0:T(4,128)}, u32[]{:S(2)}) copy-start(f32[48,4,1024]{2,1,0:T(4,128)} %fac.1) | copy-start | bytes 2359300
  0.0 38.3 %copy-start.2 = (s32[2,3]{1,0:T(2,128)S(1)}, s32[2,3]{1,0:T(2,128)}, u32[]{:S(2)}) copy-start(s32[2,3]{1,0:T(2,128)} %tri.3) | copy-start | bytes 76
  38.3 0.9 %copy-start.1 = (f32[6,4,1024]{2,1,0:T(4,128)S(1)}, f32[6,4,1024]{2,1,0:T(4,128)}, u32[]{:S(2)}) copy-start(f32[6,4,1024]{2,1,0:T(4,128)} %shard_map.46.steps) | copy-start | bytes 294916
